TPU v7x, 32 devices: a whole 2x2x4 slice. The times are simulated.
32 devices in a mesh: ia: 2 (over y), ja: 4 (over z), ka: 4 (over x, core).
Axes of the slice: x: 2, y: 2, z: 4, core: 2. Of those that a mesh axis runs over, the one named last changes fastest.
Arguments:
- blocks: bfloat16 [32, 64, 64, 128], P(('ia', 'ja', 'ka')), may hold values from -6 to 6
- coords: int32 [3, 32], P(None, ('ia', 'ja', 'ka')), may hold values from 0 to 15, as said below
- live: int32 [32], P(('ia', 'ja', 'ka')), may hold values from 1 to 1, as said below
- factor_b: float32 [1024, 128], P('ja'), may hold values from -0.9 to 12
- factor_c: float32 [2048, 128], P('ka'), may hold values from -0.9 to 12
Outputs:
- loading_a: float32 [512, 128], P('ia')
- loading_b: float32 [1024, 128], P('ja')
- loading_c: float32 [2048, 128], P('ka')
Inputs may be any that keep to these rules, and one draw needn't show every extreme that they name: `live`: slot d holds the block of device d (devices counted along ia, ja, ka, ia slowest). The slots of device (p, q, s) name blocks with coords[0] from p * 4 to p * 4 + 3, coords[1] from q * 4 to q * 4 + 3, coords[2] from s * 4 to s * 4 + 3; each device's slot names one block of its own 4 x 4 x 4 block region.
All inputs are finite; a program needn't handle non-finite values.
Results may differ from a plain program's by a relative error of at most 0.0057.
Values sent between devices are 32-bit elements; how exact they have to be, the bound alone decides.
A program may use at most 64 MiB of HBM per device.

v0:
```python
import jax
import jax.numpy as jnp
from jax import lax
from jax.sharding import PartitionSpec as P

RANK = 128
BI = 64
BJ = 64
BK = 128
GI_DEV = 4
GJ_DEV = 4
GK_DEV = 4


RIDGE_SHARE = 0.3
EPSILON = 1e-06
HIGHEST = lax.Precision.HIGHEST
sweep_order = (0, 1, 2)


def factorize(gram_one, gram_two):
    merged = gram_one * gram_two
    order_rank = merged.shape[0]
    shift_value = RIDGE_SHARE * jnp.trace(merged) / order_rank
    lower_factor = jnp.linalg.cholesky(
        merged + shift_value * jnp.eye(order_rank, dtype=jnp.float32)
    )
    return lax.linalg.triangular_solve(
        lower_factor, jnp.eye(order_rank, dtype=jnp.float32), left_side=True, lower=True
    )


def apply_inverse(inverse_lower, values):
    middle = jnp.dot(values, inverse_lower.T, precision=HIGHEST, preferred_element_type=jnp.float32)
    return jnp.dot(middle, inverse_lower, precision=HIGHEST, preferred_element_type=jnp.float32)


def square_product(values):
    return jnp.dot(values.T, values, precision=HIGHEST, preferred_element_type=jnp.float32)


def grand_sum(values):
    return lax.psum(values, ("ia", "ja", "ka"))


def move_rows(mode_now, action, values):
    if mode_now == 0:
        if action == "reduce":
            return lax.psum_scatter(values, ("ja", "ka"), scatter_dimension=0, tiled=True)
        return lax.all_gather(values, ("ja", "ka"), axis=0, tiled=True)
    if mode_now == 1:
        if action == "reduce":
            return lax.psum_scatter(values, ("ia", "ka"), scatter_dimension=0, tiled=True)
        return lax.all_gather(values, ("ia", "ka"), axis=0, tiled=True)
    if action == "reduce":
        return lax.psum_scatter(values, ("ia", "ja"), scatter_dimension=0, tiled=True)
    return lax.all_gather(values, ("ia", "ja"), axis=0, tiled=True)


def group_place(mode_now):
    if mode_now == 0:
        return (lax.axis_index(("ja", "ka")), lax.axis_size(("ja", "ka")), lax.axis_size("ia"))
    if mode_now == 1:
        return (lax.axis_index(("ia", "ka")), lax.axis_size(("ia", "ka")), lax.axis_size("ja"))
    return (lax.axis_index(("ia", "ja")), lax.axis_size(("ia", "ja")), lax.axis_size("ka"))


def share_rows(values, group_index, group_size):
    share_width = values.shape[0] // group_size
    return lax.dynamic_slice_in_dim(values, group_index * share_width, share_width, 0)


def starting_gram(values, mode_now):
    group_index, group_size, mode_size = group_place(mode_now)
    share = share_rows(values, group_index, group_size)
    return grand_sum(square_product(share)) / (values.shape[0] * mode_size)


def normalize(stat_rows, count_rows, need_gram):
    squares = lax.psum(jnp.sum(stat_rows * stat_rows, axis=0), ("ia", "ja", "ka")) / count_rows
    scale = lax.rsqrt(squares + EPSILON)
    if not need_gram:
        return (scale, None)
    scaled = stat_rows * scale
    return (scale, grand_sum(square_product(scaled)) / count_rows)


def settle(mode_now, summed, inverse_lower, need_gram):
    group_index, group_size, mode_size = group_place(mode_now)
    count_rows = summed.shape[0] * mode_size
    solved = apply_inverse(inverse_lower, move_rows(mode_now, "reduce", summed))
    scale, gram_new = normalize(solved, count_rows, need_gram)
    return (move_rows(mode_now, "spread", solved * scale), gram_new)


def block_product(mode_now, tensor_block, rows_one, rows_two):
    khatri = (rows_one[:, None, :] * rows_two[None, :, :]).astype(jnp.bfloat16)
    kept_dims = tuple((axis_id for axis_id in range(3) if axis_id != mode_now))
    return lax.dot_general(
        tensor_block, khatri, ((kept_dims, (0, 1)), ((), ())), preferred_element_type=jnp.float32
    )


def local_mttkrp(mode_now, blocks, coords, live_count, factors, bases):
    extents = (BI, BJ, BK)
    spans = (BI * GI_DEV, BJ * GJ_DEV, BK * GK_DEV)
    others = tuple((axis_id for axis_id in range(3) if axis_id != mode_now))

    def visit(slot_index, summed):
        tensor_block = lax.dynamic_index_in_dim(blocks, slot_index, 0, keepdims=False)
        start_one = (coords[others[0], slot_index] - bases[others[0]]) * extents[others[0]]
        start_two = (coords[others[1], slot_index] - bases[others[1]]) * extents[others[1]]
        rows_one = lax.dynamic_slice_in_dim(factors[others[0]], start_one, extents[others[0]], 0)
        rows_two = lax.dynamic_slice_in_dim(factors[others[1]], start_two, extents[others[1]], 0)
        product_rows = block_product(mode_now, tensor_block, rows_one, rows_two)
        offset = (coords[mode_now, slot_index] - bases[mode_now]) * extents[mode_now]
        current = lax.dynamic_slice_in_dim(summed, offset, extents[mode_now], 0)
        return lax.dynamic_update_slice_in_dim(summed, current + product_rows, offset, 0)

    start_rows = jnp.zeros((spans[mode_now], RANK), jnp.float32)
    return lax.fori_loop(0, live_count, visit, start_rows)


def on_device(blocks, coords, live, factor_b, factor_c):
    bases = (
        lax.axis_index("ia") * GI_DEV,
        lax.axis_index("ja") * GJ_DEV,
        lax.axis_index("ka") * GK_DEV,
    )
    factors = [None, factor_b, factor_c]
    gram_list = [None, starting_gram(factor_b, 1), starting_gram(factor_c, 2)]
    for position, mode_now in enumerate(sweep_order):
        others = tuple((axis_id for axis_id in range(3) if axis_id != mode_now))
        summed = local_mttkrp(mode_now, blocks, coords, live[0], factors, bases)
        inverse_lower = factorize(gram_list[others[0]], gram_list[others[1]])
        factors[mode_now], gram_list[mode_now] = settle(
            mode_now, summed, inverse_lower, position < 2
        )
    return (factors[0], factors[1], factors[2])


def solution(mesh):
    placed = (
        P(("ia", "ja", "ka"), None, None, None),
        P(None, ("ia", "ja", "ka")),
        P(("ia", "ja", "ka")),
        P("ja", None),
        P("ka", None),
    )
    return jax.shard_map(
        on_device,
        mesh=mesh,
        in_specs=placed,
        out_specs=(P("ia", None), P("ja", None), P("ka", None)),
        check_vma=False,
    )
```

profile of v0, /device:TPU:0, one launch (start us, length us, event | category | flops | bytes accessed | tf_op | source)
XLA Modules:
  0.0 658.8 jit_solution(10842126697849781549)
XLA Ops:
  8.0 0.0 all-reduce.9.cloned.1.call-start
  8.1 1.7 fusion.31
  9.8 0.9 fusion.29
  10.7 0.0 reduce-scatter.4.cloned.1.call-start
  10.8 1.4 fusion.37
  14.0 0.8 constant_dynamic-slice_fusion.3
  14.8 2.0 fusion.10
  16.8 1.4 while.42
  18.2 0.6 copy-done.2
  18.9 0.0 all-reduce.5.cloned.1.call-start
  19.0 121.7 %all-reduce.9.cloned.1.call-done = (f32[128,128]{0,1:T(8,128)}, f32[128,128]{0,1:T(8,128)}) async-done(((f32[128,128]{0,1:T(8,128)}, f32[128,128]{0,1:T(8,128)}), (f32[128,128]{0,1:T(8,128)}, f32[128,128]{0,1:T(8,128)})) %all-reduce.9.cloned.1.call-update) | async-done | bytes 131088 | tf_op jit(solution)/shard_map/psum | solution.py:43
  140.7 1.5 select_reduce_fusion.5
  142.8 0.9 select_add_fusion.2
  143.7 0.1 copy.10
  143.9 11.7 %cholesky.59 = f32[128,128]{1,0:T(8,128)S(1)} custom-call(f32[128,128]{1,0:T(8,128)S(1)} %fusion.28), custom_call_target="Cholesky" | custom-call | tf_op jit(solution)/shard_map/jit(cholesky)/cholesky | solution.py:25
  155.6 0.6 compare_reduce_fusion.2
  156.2 0.7 fusion.20
  156.9 9.8 %custom-call.7 = f32[1,128,128]{1,2,0:T(8,128)S(1)} custom-call(f32[1,128,128]{2,1,0:T(8,128)S(1)} %fusion.20), custom_call_target="InvertDiagBlocksLowerTriangular" | custom-call | tf_op jit(solution)/shard_map/triangular_solve/custom-call.0 | solution.py:28
  166.7 0.3 fusion.18
  167.1 0.9 fusion.38
  167.9 0.2 multiply_reduce_fusion.2
  168.2 39.3 %psum.51 = f32[128]{0:T(128)S(1)} all-reduce(f32[128]{0:T(128)S(1)} %get-tuple-element.553), channel_id=1, replica_groups=mesh['ia'=2,'ja'=4,'ka'=4] {'ia','ja','ka'}, use_global_device_ids=true, to_apply=%region_9.12 | all-reduce | flops 128 | bytes 1024 | tf_op jit(solution)/shard_map/psum | solution.py:80
  207.4 0.9 fusion.39
  208.4 21.4 %all_gather.9 = f32[256,128]{1,0:T(8,128)S(1)} all-gather(f32[16,128]{1,0:T(8,128)S(1)} %broadcast_multiply_fusion.2), channel_id=1, replica_groups=mesh['ia'=2,'ja'=4,'ka'=4] {'ja','ka'}, dimensions={0}, use_global_device_ids=true | all-gather | bytes 139264 | tf_op jit(solution)/shard_map/all_gather | solution.py:50
  229.8 0.0 reduce-scatter.6.cloned.1.call-start
  229.9 0.5 fusion.9
  230.4 1.3 while.43
  231.7 0.6 copy-done.3
  232.4 0.2 all-reduce.7.cloned.1.call-start
  232.6 111.2 %all-reduce.5.cloned.1.call-done = f32[128,128]{0,1:T(8,128)} async-done(((f32[128,128]{0,1:T(8,128)}), f32[128,128]{0,1:T(8,128)}) %all-reduce.5.cloned.1.call-update) | async-done | bytes 65552 | tf_op jit(solution)/shard_map/psum | solution.py:43
  343.9 1.5 select_reduce_fusion.4
  346.0 0.9 select_add_fusion.1
  346.8 0.1 copy.12
  346.9 11.7 %cholesky.70 = f32[128,128]{1,0:T(8,128)S(1)} custom-call(f32[128,128]{1,0:T(8,128)S(1)} %fusion.26), custom_call_target="Cholesky" | custom-call | tf_op jit(solution)/shard_map/jit(cholesky)/cholesky | solution.py:25
  358.7 0.6 compare_reduce_fusion.1
  359.3 0.7 fusion.21
  360.0 9.8 %custom-call.8 = f32[1,128,128]{1,2,0:T(8,128)S(1)} custom-call(f32[1,128,128]{2,1,0:T(8,128)S(1)} %fusion.21), custom_call_target="InvertDiagBlocksLowerTriangular" | custom-call | tf_op jit(solution)/shard_map/triangular_solve/custom-call.0 | solution.py:28
  369.8 0.3 fusion.16
  370.1 11.7 %reduce-scatter.6.cloned.1.call-done = f32[32,128]{1,0:T(8,128)} async-done(((f32[256,128]{1,0:T(8,128)}), f32[32,128]{1,0:T(8,128)}) %reduce-scatter.6.cloned.1.call-update) | async-done | bytes 16400 | tf_op jit(solution)/shard_map/reduce_scatter | solution.py:53
  381.8 0.9 fusion.40
  382.7 0.2 multiply_reduce_fusion.1
  383.0 39.4 %psum.53 = f32[128]{0:T(128)S(1)} all-reduce(f32[128]{0:T(128)S(1)} %get-tuple-element.555), channel_id=1, replica_groups=mesh['ia'=2,'ja'=4,'ka'=4] {'ia','ja','ka'}, use_global_device_ids=true, to_apply=%region_16.19 | all-reduce | flops 128 | bytes 1024 | tf_op jit(solution)/shard_map/psum | solution.py:80
  422.3 0.9 fusion.41
  423.3 10.0 %all_gather.10 = f32[256,128]{1,0:T(8,128)S(1)} all-gather(f32[32,128]{1,0:T(8,128)S(1)} %broadcast_multiply_fusion.1), channel_id=1, replica_groups=mesh['ia'=2,'ja'=4,'ka'=4] {'ia','ka'}, dimensions={0}, use_global_device_ids=true | all-gather | bytes 147456 | tf_op jit(solution)/shard_map/all_gather | solution.py:54
  433.2 0.0 reduce-scatter.8.cloned.1.call-start
  433.3 0.5 convolution_bitcast_fusion
  433.9 1.6 while.44
  435.5 0.7 copy-done.1
  436.2 113.9 %all-reduce.7.cloned.1.call-done = f32[128,128]{0,1:T(8,128)} async-done(((f32[128,128]{0,1:T(8,128)}), f32[128,128]{0,1:T(8,128)}) %all-reduce.7.cloned.1.call-update) | async-done | bytes 65552 | tf_op jit(solution)/shard_map/psum | solution.py:43
  550.0 1.5 select_reduce_fusion.3
  552.2 0.9 select_add_fusion
  553.0 0.1 copy.14
  553.1 11.7 %cholesky.81 = f32[128,128]{1,0:T(8,128)S(1)} custom-call(f32[128,128]{1,0:T(8,128)S(1)} %fusion.24), custom_call_target="Cholesky" | custom-call | tf_op jit(solution)/shard_map/jit(cholesky)/cholesky | solution.py:25
  564.9 0.6 compare_reduce_fusion
  565.5 0.7 fusion.22
  566.2 9.8 %custom-call.9 = f32[1,128,128]{1,2,0:T(8,128)S(1)} custom-call(f32[1,128,128]{2,1,0:T(8,128)S(1)} %fusion.22), custom_call_target="InvertDiagBlocksLowerTriangular" | custom-call | tf_op jit(solution)/shard_map/triangular_solve/custom-call.0 | solution.py:28
  576.0 0.3 fusion.14
  576.3 1.0 fusion.42
  577.3 0.2 multiply_reduce_fusion
  577.5 40.9 %psum.55 = f32[128]{0:T(128)S(1)} all-reduce(f32[128]{0:T(128)S(1)} %get-tuple-element.557), channel_id=1, replica_groups=mesh['ia'=2,'ja'=4,'ka'=4] {'ia','ja','ka'}, use_global_device_ids=true, to_apply=%region_23.26 | all-reduce | flops 128 | bytes 1024 | tf_op jit(solution)/shard_map/psum | solution.py:80
  618.4 31.2 %all_gather.11 = f32[512,128]{1,0:T(8,128)S(1)} all-gather(f32[64,128]{1,0:T(8,128)S(1)} %broadcast_multiply_fusion), channel_id=1, replica_groups=mesh['ia'=2,'ja'=4,'ka'=4] {'ia','ja'}, dimensions={0}, use_global_device_ids=true | all-gather | bytes 294912 | tf_op jit(solution)/shard_map/all_gather | solution.py:57
  649.7 0.7 copy.52
  650.3 0.7 copy.53
  651.0 0.7 copy.54
  (40 shorter events, 0.5 us)
Async XLA Ops:
  8.0 1.8 copy-start
  8.0 132.7 %all-reduce.9.cloned.1.call-start = ((), (), s32[]{:S(2)}) async-start(), calls=%async_computation.8 | async-start | bytes 262144 | tf_op jit(solution)/shard_map/psum | solution.py:43
  10.7 156.3 %reduce-scatter.4.cloned.1.call-start = ((), (), s32[]{:S(2)}) async-start(), calls=%async_computation.3 | async-start | bytes 139264 | tf_op jit(solution)/shard_map/reduce_scatter | solution.py:49
  16.8 213.1 %copy-start.6 = (bf16[1,64,64,128]{3,2,1,0:T(8,128)(2,1)S(1)}, bf16[1,64,64,128]{3,2,1,0:T(8,128)(2,1)}, u32[]{:S(2)}) copy-start(bf16[1,64,64,128]{3,2,1,0:T(8,128)(2,1)} %param.14) | copy-start | bytes 3145732
  18.2 0.7 copy-start.2
  18.9 324.9 %all-reduce.5.cloned.1.call-start = ((), (), s32[]{:S(2)}) async-start(), calls=%async_computation.5 | async-start | bytes 131072 | tf_op jit(solution)/shard_map/psum | solution.py:43
  229.8 152.0 %reduce-scatter.6.cloned.1.call-start = ((), (), s32[]{:S(2)}) async-start(), calls=%async_computation.4 | async-start | bytes 147456 | tf_op jit(solution)/shard_map/reduce_scatter | solution.py:53
  229.9 114.0 %copy-start.4 = (f32[128,128]{0,1:T(8,128)S(1)}, f32[128,128]{0,1:T(8,128)}, u32[]{:S(2)}) copy-start(f32[128,128]{0,1:T(8,128)} %get-tuple-element.548) | copy-start | bytes 196612
  231.7 0.7 copy-start.3
  232.4 317.6 %all-reduce.7.cloned.1.call-start = ((), (), s32[]{:S(2)}) async-start(), calls=%async_computation.7 | async-start | bytes 131072 | tf_op jit(solution)/shard_map/psum | solution.py:43
  433.2 143.1 %reduce-scatter.8.cloned.1.call-start = ((), (), s32[]{:S(2)}) async-start(), calls=%async_computation.6 | async-start | bytes 294912 | tf_op jit(solution)/shard_map/reduce_scatter | solution.py:56
  433.8 116.2 %copy-start.5 = (f32[128,128]{0,1:T(8,128)S(1)}, f32[128,128]{0,1:T(8,128)}, u32[]{:S(2)}) copy-start(f32[128,128]{0,1:T(8,128)} %all-reduce.5.cloned.1.call-done) | copy-start | bytes 196612
  435.4 0.7 copy-start.1
Sparse Core Ops, SparseCore 0:
  15.1 125.5 all-reduce.8
  229.9 113.8 all-reduce.4
  347.4 34.3 reduce-scatter.5
  433.4 116.6 all-reduce.6
Sparse Core Ops, SparseCore 1:
  19.0 57.8 reduce-scatter.3
  438.0 60.5 reduce-scatter.7
where the time goes:
time: 660 us; the launch traced here: 659 us
  waiting for transfers between devices  359 us (54%)
  blocking collectives  182 us (28%)
  other arithmetic  75.7 us (11%)
  between operations  19.3 us (3%)
  matrix products  11.7 us (2%)
    psum x3, waiting for transfers between devices, grand_sum(): return lax.psum(values, ('ia', 'ja', 'ka'))  347 us
    psum x3, blocking collectives, normalize(): lax.psum(jnp.sum(stat_rows * stat_rows, axis=0), ('ia', 'ja', 'ka'))  119 us
    another operation x9, other arithmetic, factorize(): jnp.linalg.cholesky(merged + shift_value * jnp.eye(order_rank, dtype=jnp....  37.2 us
    another operation x6, other arithmetic, factorize(): lax.linalg.triangular_solve(lower_factor, jnp.eye(order_rank, dtype=jnp.f...  31.4 us
    all_gather x1, blocking collectives, move_rows(): return lax.all_gather(values, ('ia', 'ja'), axis=0, tiled=True)  31.2 us
    all_gather x1, blocking collectives, move_rows(): return lax.all_gather(values, ('ja', 'ka'), axis=0, tiled=True)  21.4 us
  transfers between devices with their start and end apart: 6, of which 4 were waited for; matrix products, arithmetic and copies ran while one was open for 12% of the time, Pallas kernels for 0%

commit v1 on v0

v1 whole, which is shorter than its diff:
```python
import functools

import jax
import jax.numpy as jnp
from jax import lax
from jax.experimental import pallas as pl
from jax.experimental.pallas import tpu as pltpu
from jax.sharding import PartitionSpec as P

GI_DEV = 4
RIDGE_SHARE = 0.3
EPSILON = 1e-06
HIGHEST = lax.Precision.HIGHEST
MESH = pl.DeviceIdType.MESH
F32 = jnp.float32
BF16 = jnp.bfloat16
CHUNK = 8


def newton_plan(order):
    low = RIDGE_SHARE / order
    high = 1.0 + low
    first = 2.0 / (low + high)
    error = (high - low) / (high + low)
    scales = []
    while error > 1e-9:
        square = error * error
        scales.append(2.0 / (2.0 - square))
        error = square / (2.0 - square)
    return first, scales


def dot_high(left, right):
    return jnp.dot(left, right, precision=HIGHEST, preferred_element_type=F32)


def system_inverse(gram_one, gram_two):
    order = gram_one.shape[0]
    merged = gram_one * gram_two
    on_diagonal = lax.broadcasted_iota(jnp.int32, (order, order), 0) == lax.broadcasted_iota(
        jnp.int32, (order, order), 1
    )
    eye = jnp.where(on_diagonal, 1.0, 0.0).astype(F32)
    trace = jnp.sum(jnp.sum(merged * eye, axis=1, keepdims=True), axis=0, keepdims=True)
    unit = 1.0 / trace
    system = merged * unit + (RIDGE_SHARE / order) * eye
    first, scales = newton_plan(order)
    twice = 2.0 * eye
    guess = (scales[0] * first) * (twice - first * system)
    for scale in scales[1:]:
        residual = twice - dot_high(system, guess)
        guess = scale * dot_high(guess, residual)
    return guess * unit


def gram_of(values):
    return lax.dot_general(
        values, values, (((0,), (0,)), ((), ())), precision=HIGHEST, preferred_element_type=F32
    )


def kernel(
    sizes,
    coords,
    tensor,
    factor_b,
    factor_c,
    out_a,
    out_b,
    out_c,
    wide,
    turned,
    rows_one,
    gram_b_buf,
    gram_c_buf,
    send_0,
    send_1,
    send_2,
    take_0,
    take_1,
    take_2,
    share_0,
    share_1,
    share_2,
    sums,
    gram_b_sems,
    gram_c_sems,
    cut_sems_0,
    cut_sems_1,
    cut_sems_2,
    spread_sems_0,
    spread_sems_1,
    spread_sems_2,
    sum_sems,
):
    n_i, n_j, n_k = sizes
    n_all = n_i * n_j * n_k
    p, q, s = lax.axis_index("ia"), lax.axis_index("ja"), lax.axis_index("ka")
    me = (p * n_j + q) * n_k + s
    spans = (out_a.shape[0], out_b.shape[0], out_c.shape[0])
    extents = (turned.shape[1], turned.shape[0], turned.shape[2])
    counts = tuple(span // extent for span, extent in zip(spans, extents))

    def everyone(index):
        return (index // (n_j * n_k), (index // n_k) % n_j, index % n_k)

    groups = (
        (n_j * n_k, q * n_k + s, lambda u: (p, u // n_k, u % n_k)),
        (n_i * n_k, p * n_k + s, lambda u: (u // n_k, q, u % n_k)),
        (n_i * n_j, p * n_j + q, lambda u: (u // n_j, u % n_j, s)),
    )
    all_group = (n_all, me, everyone)
    ja_group = (n_j, q, lambda u: (p, u, s))
    ka_group = (n_k, s, lambda u: (p, q, u))

    def partners(group, body):
        size, mine, place = group

        @pl.loop(1, size)
        def _(offset):
            other = lax.rem(mine + offset, size)
            body(other, place(other))

    def copy(source, target, sems, mine, other, device):
        return pltpu.make_async_remote_copy(
            src_ref=source,
            dst_ref=target,
            send_sem=sems.at[0, other],
            recv_sem=sems.at[1, mine],
            device_id=device,
            device_id_type=MESH,
        )

    def spread(group, buffer, sems):
        mine = group[1]

        def body(other, device):
            copy(buffer.at[mine], buffer.at[mine], sems, mine, other, device).start()

        partners(group, body)

    def arrive(group, buffer, sems):
        def body(other, device):
            copy(buffer.at[other], buffer.at[other], sems, other, other, device).wait_recv()

        partners(group, body)

    def sent(group, buffer, sems):
        mine = group[1]

        def body(other, device):
            copy(buffer.at[mine], buffer.at[mine], sems, mine, other, device).wait_send()

        partners(group, body)

    barrier = pltpu.get_barrier_semaphore()

    def greet(other, device):
        pl.semaphore_signal(barrier, inc=1, device_id=device, device_id_type=MESH)

    partners(all_group, greet)
    gram_b_buf[q] = gram_of(factor_b[...])
    gram_c_buf[s] = gram_of(factor_c[...])
    pl.semaphore_wait(barrier, n_all - 1)
    spread(ja_group, gram_b_buf, gram_b_sems)
    spread(ka_group, gram_c_buf, gram_c_sems)

    def marks_of(mode, base):
        row = lax.broadcasted_iota(jnp.int32, (counts[mode], out_a.shape[1]), 0) + base
        return jnp.where(row == jnp.full(row.shape, coords[mode, 0], jnp.int32), 1.0, 0.0)

    marks = (marks_of(0, p * counts[0]), marks_of(1, q * counts[1]), marks_of(2, s * counts[2]))

    def block_rows(mode, source):
        extent = extents[mode]
        return sum(
            source[g * extent : (g + 1) * extent, :] * marks[mode][g : g + 1, :]
            for g in range(counts[mode])
        )

    wide[...] = tensor[...].astype(F32)

    @pl.loop(0, extents[1])
    def _(b):
        turned[b] = wide[pl.ds(b, extents[0], stride=extents[1]), :].astype(BF16)

    def product(mode, rows_of_one, rows_of_two):
        rows_one[0 : rows_of_one.shape[0], :] = rows_of_one
        total = jnp.zeros((extents[mode], rows_of_two.shape[1]), F32)

        def step(j, total):
            ones = rows_one[pl.ds(pl.multiple_of(j * CHUNK, CHUNK), CHUNK), :]
            khatri = jnp.concatenate(
                [(ones[i : i + 1, :] * rows_of_two).astype(BF16) for i in range(CHUNK)], axis=0
            )
            if mode == 2:
                depth = CHUNK * extents[1]
                left = tensor[pl.ds(pl.multiple_of(j * depth, depth), depth), :]
                dims = (((0,), (0,)), ((), ()))
            else:
                if mode == 0:
                    parts = [turned[j * CHUNK + i] for i in range(CHUNK)]
                else:
                    parts = [
                        tensor[pl.ds(pl.multiple_of((j * CHUNK + i) * extents[1], extents[1]), extents[1]), :]
                        for i in range(CHUNK)
                    ]
                left = jnp.concatenate(parts, axis=1)
                dims = (((1,), (0,)), ((), ()))
            return total + lax.dot_general(left, khatri, dims, preferred_element_type=F32)

        return lax.fori_loop(0, rows_of_one.shape[0] // CHUNK, step, total)

    def cut(mode, rows, send, take, sems):
        size, mine, _ = groups[mode]
        share = extents[mode] // size
        for u in range(size):
            send[u, 0:share, :] = rows[u * share : (u + 1) * share, :]
            send[u, share : share + counts[mode], :] = marks[mode]

        def body(other, device):
            copy(send.at[other], take.at[mine], sems, mine, other, device).start()

        partners(groups[mode], body)

    def gather_cut(mode, send, take, sems):
        size, mine, _ = groups[mode]
        share, count = extents[mode] // size, counts[mode]

        def add(total, buffer, index):
            rows = buffer[index, 0:share, :]
            return tuple(
                total[g] + rows * buffer[index, share + g : share + g + 1, :] for g in range(count)
            )

        total = tuple(jnp.zeros((share, out_a.shape[1]), F32) for _ in range(count))
        total = add(total, send, mine)

        def body(offset, total):
            other = lax.rem(mine + offset, size)
            place = groups[mode][2](other)
            copy(send.at[other], take.at[other], sems, other, other, place).wait_recv()
            return add(total, take, other)

        total = lax.fori_loop(1, size, body, total)
        return jnp.concatenate(total, axis=0)

    def cut_sent(mode, send, take, sems):
        mine = groups[mode][1]

        def body(other, device):
            copy(send.at[other], take.at[mine], sems, mine, other, device).wait_send()

        partners(groups[mode], body)

    def place_rows(mode, out, buffer, slot_of, scale):
        size = groups[mode][0]
        share = extents[mode] // size
        for u in range(size):
            rows = buffer[slot_of(u)] * scale
            for g in range(counts[mode]):
                start = g * extents[mode] + u * share
                out[start : start + share, :] = rows[g * share : (g + 1) * share, :]

    lengths = (spans[0] * n_i, spans[1] * n_j, spans[2] * n_k)

    def finish(mode, shares, out, slot_of):
        rows = shares[...].reshape(lengths[mode], out.shape[1])
        squares = jnp.sum(rows * rows, axis=0, keepdims=True) / lengths[mode]
        scale = lax.rsqrt(squares + EPSILON)
        place_rows(mode, out, shares, slot_of, scale)
        return gram_of(rows * scale) / lengths[mode]

    rows = product(0, block_rows(1, factor_b), block_rows(2, factor_c))
    cut(0, rows, send_0, take_0, cut_sems_0)
    arrive(ja_group, gram_b_buf, gram_b_sems)
    arrive(ka_group, gram_c_buf, gram_c_sems)
    gram_b = jnp.sum(gram_b_buf[...], axis=0) / lengths[1]
    gram_c = jnp.sum(gram_c_buf[...], axis=0) / lengths[2]
    inverse = system_inverse(gram_b, gram_c)
    share_0[me] = dot_high(gather_cut(0, send_0, take_0, cut_sems_0), inverse)
    spread(all_group, share_0, spread_sems_0)
    arrive(all_group, share_0, spread_sems_0)
    gram_a = finish(0, share_0, out_a, lambda u: p * groups[0][0] + u)

    rows = product(1, block_rows(0, out_a), block_rows(2, factor_c))
    cut(1, rows, send_1, take_1, cut_sems_1)
    inverse = system_inverse(gram_a, gram_c)
    share_1[me] = dot_high(gather_cut(1, send_1, take_1, cut_sems_1), inverse)
    spread(all_group, share_1, spread_sems_1)
    arrive(all_group, share_1, spread_sems_1)
    gram_b = finish(1, share_1, out_b, lambda u: ((u // n_k) * n_j + q) * n_k + u % n_k)

    rows = product(2, block_rows(0, out_a), block_rows(1, out_b))
    cut(2, rows, send_2, take_2, cut_sems_2)
    inverse = system_inverse(gram_a, gram_b)
    solved = dot_high(gather_cut(2, send_2, take_2, cut_sems_2), inverse)
    mine = groups[2][1]
    share_2[mine] = solved
    sums[me] = jnp.broadcast_to(jnp.sum(solved * solved, axis=0, keepdims=True), sums.shape[1:])
    spread(all_group, sums, sum_sems)
    spread(groups[2], share_2, spread_sems_2)
    arrive(all_group, sums, sum_sems)
    arrive(groups[2], share_2, spread_sems_2)
    squares = jnp.sum(sums[...], axis=0)[0:1, :] / lengths[2]
    place_rows(2, out_c, share_2, lambda u: u, lax.rsqrt(squares + EPSILON))

    sent(ja_group, gram_b_buf, gram_b_sems)
    sent(ka_group, gram_c_buf, gram_c_sems)
    cut_sent(0, send_0, take_0, cut_sems_0)
    cut_sent(1, send_1, take_1, cut_sems_1)
    cut_sent(2, send_2, take_2, cut_sems_2)
    sent(all_group, share_0, spread_sems_0)
    sent(all_group, share_1, spread_sems_1)
    sent(groups[2], share_2, spread_sems_2)
    sent(all_group, sums, sum_sems)


def on_device(sizes, blocks, coords, live, factor_b, factor_c):
    n_i, n_j, n_k = sizes
    n_all = n_i * n_j * n_k
    slots, bi, bj, bk = blocks.shape
    rank = factor_b.shape[1]
    span_a, span_b, span_c = GI_DEV * bi, factor_b.shape[0], factor_c.shape[0]
    group_sizes = (n_j * n_k, n_i * n_k, n_i * n_j)
    spans = (span_a, span_b, span_c)
    extents = (bi, bj, bk)

    def message(mode):
        rows = extents[mode] // group_sizes[mode] + spans[mode] // extents[mode]
        return (group_sizes[mode], (rows + 7) // 8 * 8, rank)

    def buffer(*shape):
        return pltpu.VMEM(shape, F32)

    vmem = pl.BlockSpec(memory_space=pltpu.VMEM)
    return pl.pallas_call(
        functools.partial(kernel, sizes),
        out_shape=[jax.ShapeDtypeStruct((span, rank), F32) for span in spans],
        in_specs=[pl.BlockSpec(memory_space=pltpu.SMEM), vmem, vmem, vmem],
        out_specs=[vmem] * 3,
        scratch_shapes=[
            buffer(bi * bj, bk),
            pltpu.VMEM((bj, bi, bk), BF16),
            buffer(max(bi, bj), rank),
            buffer(n_j, rank, rank),
            buffer(n_k, rank, rank),
            *[buffer(*message(mode)) for mode in range(3)],
            *[buffer(*message(mode)) for mode in range(3)],
            buffer(n_all, span_a // group_sizes[0], rank),
            buffer(n_all, span_b // group_sizes[1], rank),
            buffer(group_sizes[2], span_c // group_sizes[2], rank),
            buffer(n_all, 8, rank),
            pltpu.SemaphoreType.DMA((2, n_j)),
            pltpu.SemaphoreType.DMA((2, n_k)),
            *[pltpu.SemaphoreType.DMA((2, size)) for size in group_sizes],
            pltpu.SemaphoreType.DMA((2, n_all)),
            pltpu.SemaphoreType.DMA((2, n_all)),
            pltpu.SemaphoreType.DMA((2, group_sizes[2])),
            pltpu.SemaphoreType.DMA((2, n_all)),
        ],
        compiler_params=pltpu.CompilerParams(
            collective_id=0, has_side_effects=True, vmem_limit_bytes=40 * 1024 * 1024
        ),
    )(coords, blocks.reshape(slots * bi * bj, bk), factor_b, factor_c)


def solution(mesh):
    sizes = (mesh.shape["ia"], mesh.shape["ja"], mesh.shape["ka"])
    placed = (
        P(("ia", "ja", "ka"), None, None, None),
        P(None, ("ia", "ja", "ka")),
        P(("ia", "ja", "ka")),
        P("ja", None),
        P("ka", None),
    )
    return jax.shard_map(
        functools.partial(on_device, sizes),
        mesh=mesh,
        in_specs=placed,
        out_specs=(P("ia", None), P("ja", None), P("ka", None)),
        check_vma=False,
    )
```

time: 660 us -> 73.6 us (0.11)
  waiting for transfers between devices: 359 us -> 0 us
  blocking collectives: 182 us -> 0 us
  other arithmetic: 75.7 us -> 0 us
  Pallas kernels: 0 us -> 66.9 us
  between operations: 19.3 us -> 0.65 us
  matrix products: 11.7 us -> 0 us
    psum x3 -> x0, waiting for transfers between devices: 347 us -> none  [grand_sum(): return lax.psum(values, ('ia', 'ja', 'ka'))]
    psum x3 -> x0, blocking collectives: 119 us -> none  [normalize(): lax.psum(jnp.sum(stat_rows * stat_rows, axis=0), ('ia', 'ja', 'ka'))]
    another operation x15 -> x0, other arithmetic: 68.6 us -> none  [the longest x9 37.2 us: factorize(): jnp.linalg.cholesky(merged + shift_value * jnp.eye(order_rank, dtype=jnp....]
    pallas_call x0 -> x1, Pallas kernels: none -> 66.9 us  [on_device(): pl.pallas_call(functools.partial(kernel, sizes), out_shape=[jax.ShapeDtyp...]
    all_gather x3 -> x0, blocking collectives: 62.6 us -> none  [the longest x1 31.2 us: move_rows(): return lax.all_gather(values, ('ia', 'ja'), axis=0, tiled=True)]
    reduce_scatter x3 -> x0, waiting for transfers between devices: 11.8 us -> none  [the longest x1 11.7 us: move_rows(): lax.psum_scatter(values, ('ia', 'ka'), scatter_dimension=0, tiled=True)]
    dot_general x13 -> x0, matrix products: 10.9 us -> none  [the longest x4 4.5 us: square_product(): jnp.dot(values.T, values, precision=HIGHEST, preferred_element_type=jnp.f...]
  transfers between devices with their start and end apart: 6 -> 0, of which waited for: 4 -> 0; matrix products, arithmetic and copies ran while one was open for 12% -> 0% of each run, Pallas kernels for 0% -> 0%
where the time goes in v1:
time: 73.6 us; the launch traced here: 73.4 us
  Pallas kernels  66.9 us (91%)
  local copies, waits for them, and re-layouts  5.83 us (8%)
    pallas_call x1, Pallas kernels, on_device(): pl.pallas_call(functools.partial(kernel, sizes), out_shape=[jax.ShapeDtyp...  66.9 us
    unnamed x12, local copies, waits for them, and re-layouts  5.83 us

profile of v1, /device:TPU:0, one launch (start us, length us, event | category | flops | bytes accessed | tf_op | source)
XLA Modules:
  0.0 73.4 jit_solution(482148634075061629)
XLA Ops:
  0.6 0.0 copy-start.3
  0.6 0.6 copy-done.3
  1.3 0.1 copy.7.coords
  1.4 0.0 copy-start
  1.4 1.2 %copy-done = bf16[1,64,64,128]{3,2,1,0:T(8,128)(2,1)S(1)} copy-done((bf16[1,64,64,128]{3,2,1,0:T(8,128)(2,1)S(1)}, bf16[1,64,64,128]{3,2,1,0:T(8,128)(2,1)}, u32[]{:S(2)}) %copy-start) | copy-done | bytes 1048600
  2.6 0.0 copy-start.1
  2.6 0.9 %copy-done.1 = f32[512,128]{1,0:T(8,128)S(1)} copy-done((f32[512,128]{1,0:T(8,128)S(1)}, f32[512,128]{1,0:T(8,128)}, u32[]{:S(2)}) %copy-start.1) | copy-done | bytes 262168
  3.6 0.0 copy-start.2
  3.6 0.9 %copy-done.2 = f32[256,128]{1,0:T(8,128)S(1)} copy-done((f32[256,128]{1,0:T(8,128)S(1)}, f32[256,128]{1,0:T(8,128)}, u32[]{:S(2)}) %copy-start.2) | copy-done | bytes 131096
  4.5 66.9 %shard_map.67 = (f32[256,128]{1,0:T(8,128)S(1)}, f32[256,128]{1,0:T(8,128)S(1)}, f32[512,128]{1,0:T(8,128)S(1)}) custom-call(s32[3,1]{1,0:T(4,128)S(1)} %copy.7.coords, bf16[4096,128]{1,0:T(8,128)(2,1)S(1)} %bitcast.1, f32[256,128]{1,0:T(8,128)S(1)} %copy-done.2, f32[512,128]{1,0:T(8,128)S(1)} %copy-done.1), custom_call_target="tpu_custom_call" | custom-call | tf_op jit(solution)/shard_map/pallas_call | solution.py:337
  71.3 0.7 copy.11
  72.0 0.7 copy.12
  72.7 0.7 copy.13
Async XLA Ops:
  0.6 0.7 copy-start.3
  1.4 1.2 %copy-start = (bf16[1,64,64,128]{3,2,1,0:T(8,128)(2,1)S(1)}, bf16[1,64,64,128]{3,2,1,0:T(8,128)(2,1)}, u32[]{:S(2)}) copy-start(bf16[1,64,64,128]{3,2,1,0:T(8,128)(2,1)} %param.5) | copy-start | bytes 3145732
  2.6 0.9 %copy-start.1 = (f32[512,128]{1,0:T(8,128)S(1)}, f32[512,128]{1,0:T(8,128)}, u32[]{:S(2)}) copy-start(f32[512,128]{1,0:T(8,128)} %factor_c.1) | copy-start | bytes 786436
  3.6 0.9 %copy-start.2 = (f32[256,128]{1,0:T(8,128)S(1)}, f32[256,128]{1,0:T(8,128)}, u32[]{:S(2)}) copy-start(f32[256,128]{1,0:T(8,128)} %factor_b.1) | copy-start | bytes 393220

commit v2 on v1

v2 whole, which is shorter than its diff:
```python
import functools

import jax
import jax.numpy as jnp
from jax import lax
from jax.experimental import pallas as pl
from jax.experimental.pallas import tpu as pltpu
from jax.sharding import PartitionSpec as P

GI_DEV = 4
RIDGE_SHARE = 0.3
EPSILON = 1e-06
HIGHEST = lax.Precision.HIGHEST
MESH = pl.DeviceIdType.MESH
F32 = jnp.float32
BF16 = jnp.bfloat16
CHUNK = 8


def newton_plan(order):
    low = RIDGE_SHARE / order
    high = 1.0 + low
    first = 2.0 / (low + high)
    error = (high - low) / (high + low)
    scales = []
    while error > 1e-9:
        square = error * error
        scales.append(2.0 / (2.0 - square))
        error = square / (2.0 - square)
    return first, scales


def dot_high(left, right):
    return jnp.dot(left, right, precision=HIGHEST, preferred_element_type=F32)


def halves(values):
    head = values.astype(BF16)
    return head, (values - head.astype(F32)).astype(BF16)


def dot_middle(left, right):
    left_head, left_tail = halves(left)
    right_head, right_tail = halves(right)

    def times(one, two):
        return jnp.dot(one, two, preferred_element_type=F32)

    return times(left_head, right_head) + (
        times(left_head, right_tail) + times(left_tail, right_head)
    )


def system_inverse(gram_one, gram_two):
    order = gram_one.shape[0]
    merged = gram_one * gram_two
    on_diagonal = lax.broadcasted_iota(jnp.int32, (order, order), 0) == lax.broadcasted_iota(
        jnp.int32, (order, order), 1
    )
    eye = jnp.where(on_diagonal, 1.0, 0.0).astype(F32)
    trace = jnp.sum(jnp.sum(merged * eye, axis=1, keepdims=True), axis=0, keepdims=True)
    unit = 1.0 / trace
    system = merged * unit + (RIDGE_SHARE / order) * eye
    first, scales = newton_plan(order)
    twice = 2.0 * eye
    guess = (scales[0] * first) * (twice - first * system)
    for step, scale in enumerate(scales[1:], 1):
        times = dot_high if step + 2 >= len(scales) else dot_middle
        residual = twice - times(system, guess)
        guess = scale * times(guess, residual)
    return guess * unit


def gram_of(values):
    return lax.dot_general(
        values, values, (((0,), (0,)), ((), ())), precision=HIGHEST, preferred_element_type=F32
    )


def kernel(
    sizes,
    coords,
    tensor_hbm,
    factor_b_hbm,
    factor_c_hbm,
    out_a,
    out_b,
    out_c,
    tensor,
    factor_b,
    factor_c,
    wide,
    turned,
    rows_one,
    plane_b,
    slices_b,
    whole_b,
    gram_c_buf,
    plane_a_buf,
    plane_2,
    slices_2,
    whole_2,
    send_0,
    send_1,
    send_2,
    take_0,
    take_1,
    take_2,
    share_0,
    share_1,
    share_2,
    sums_0,
    sums_1,
    sums_2,
    load_sems,
    sems,
):
    n_i, n_j, n_k = sizes
    n_all = n_i * n_j * n_k
    p, q, s = lax.axis_index("ia"), lax.axis_index("ja"), lax.axis_index("ka")
    spans = (out_a.shape[0], out_b.shape[0], out_c.shape[0])
    extents = (turned.shape[1], turned.shape[0], turned.shape[2])
    counts = tuple(span // extent for span, extent in zip(spans, extents))
    lengths = (spans[0] * n_i, spans[1] * n_j, spans[2] * n_k)
    rank = out_a.shape[1]

    loads = [
        pltpu.make_async_copy(source, target, load_sems.at[i])
        for i, (source, target) in enumerate(
            ((factor_b_hbm, factor_b), (factor_c_hbm, factor_c), (tensor_hbm, tensor))
        )
    ]
    for load in loads:
        load.start()

    position = (p, q, s)
    shifted = [
        [lax.rem(place + offset, size) for offset in range(size)]
        for place, size in zip(position, sizes)
    ]

    class Group:
        def __init__(self, *axes):
            self.axes = axes
            self.size = 1
            self.mine = 0
            for axis in axes:
                self.size *= sizes[axis]
                self.mine = self.mine * sizes[axis] + position[axis]

        def partners(self, body):
            if self.size <= 32:
                for offset in range(1, self.size):
                    device, other, rest = list(position), 0, []
                    for axis in reversed(self.axes):
                        rest.append(offset % sizes[axis])
                        offset //= sizes[axis]
                    for axis, step in zip(self.axes, reversed(rest)):
                        device[axis] = shifted[axis][step]
                        other = other * sizes[axis] + device[axis]
                    body(other, tuple(device))
            else:

                @pl.loop(1, self.size)
                def _(offset):
                    other = lax.rem(self.mine + offset, self.size)
                    device, rest = list(position), other
                    for axis in reversed(self.axes):
                        device[axis] = lax.rem(rest, sizes[axis])
                        rest = rest // sizes[axis]
                    body(other, tuple(device))

    everyone = Group(0, 1, 2)
    groups = (Group(1, 2), Group(0, 2), Group(0, 1))
    lines = (Group(0), Group(1), Group(2))
    me = everyone.mine

    def copy(source, target, phase, device):
        return pltpu.make_async_remote_copy(
            src_ref=source,
            dst_ref=target,
            send_sem=sems.at[0, phase],
            recv_sem=sems.at[1, phase],
            device_id=device,
            device_id_type=MESH,
        )

    def all_but_one(group, buffer, phase):
        part = buffer.at[pl.ds(0, group.size - 1)]
        return copy(part, part, phase, tuple(row[-1] for row in shifted))

    def spread(group, buffer, phase):
        slot = buffer.at[group.mine]
        group.partners(lambda other, device: copy(slot, slot, phase, device).start())

    def deal(group, source, target, phase):
        group.partners(
            lambda other, device: copy(
                source.at[other], target.at[group.mine], phase, device
            ).start()
        )

    def arrive(group, buffer, phase):
        all_but_one(group, buffer, phase).wait_recv()

    def sent(group, buffer, phase):
        all_but_one(group, buffer, phase).wait_send()

    barrier = pltpu.get_barrier_semaphore()
    everyone.partners(
        lambda other, device: pl.semaphore_signal(
            barrier, inc=1, device_id=device, device_id_type=MESH
        )
    )

    def store_slices(gram, plane):
        share = plane.shape[1]
        for u in range(plane.shape[0]):
            plane[u] = gram[u * share : (u + 1) * share, :]

    def start_slices(gram, plane, slices, phase):
        store_slices(gram, plane)
        mine = plane.at[groups[1].mine]
        target = slices.at[q]
        lines[1].partners(lambda other, device: copy(mine, target, phase, device).start())

    def turn_slices(plane, slices, whole, phase):
        arrive(lines[1], slices, phase)
        slices[q] = plane[groups[1].mine]
        whole[groups[1].mine] = jnp.sum(slices[...], axis=0)
        spread(groups[1], whole, phase + 1)

    def end_slices(whole, phase):
        arrive(groups[1], whole, phase + 1)
        return whole[...].reshape(rank, rank) / lengths[1]

    loads[0].wait()
    first_gram_b = gram_of(factor_b[...])
    loads[1].wait()
    gram_c_buf[s] = gram_of(factor_c[...])
    pl.semaphore_wait(barrier, n_all - 1)
    start_slices(first_gram_b, plane_b, slices_b, 0)
    spread(lines[2], gram_c_buf, 2)

    def marks_of(mode, base):
        row = lax.broadcasted_iota(jnp.int32, (counts[mode], rank), 0) + base
        return jnp.where(row == jnp.full(row.shape, coords[mode], jnp.int32), 1.0, 0.0)

    marks = (marks_of(0, p * counts[0]), marks_of(1, q * counts[1]), marks_of(2, s * counts[2]))

    def block_rows(mode, source):
        extent = extents[mode]
        return sum(
            source[g * extent : (g + 1) * extent, :] * marks[mode][g : g + 1, :]
            for g in range(counts[mode])
        )

    loads[2].wait()
    wide[...] = tensor[...].astype(F32)

    @pl.loop(0, extents[1], unroll=8)
    def _(b):
        turned[b] = wide[pl.ds(b, extents[0], stride=extents[1]), :].astype(BF16)

    def product(mode, rows_of_one, rows_of_two):
        rows_one[0 : rows_of_one.shape[0], :] = rows_of_one
        total = jnp.zeros((extents[mode], rank), F32)

        def step(j, total):
            ones = rows_one[pl.ds(pl.multiple_of(j * CHUNK, CHUNK), CHUNK), :]
            khatri = jnp.concatenate(
                [(ones[i : i + 1, :] * rows_of_two).astype(BF16) for i in range(CHUNK)], axis=0
            )
            if mode == 2:
                depth = CHUNK * extents[1]
                left = tensor[pl.ds(pl.multiple_of(j * depth, depth), depth), :]
                dims = (((0,), (0,)), ((), ()))
            else:
                if mode == 0:
                    parts = [turned[j * CHUNK + i] for i in range(CHUNK)]
                else:
                    height = extents[1]
                    parts = [
                        tensor[pl.ds(pl.multiple_of((j * CHUNK + i) * height, height), height), :]
                        for i in range(CHUNK)
                    ]
                left = jnp.concatenate(parts, axis=1)
                dims = (((1,), (0,)), ((), ()))
            return total + lax.dot_general(left, khatri, dims, preferred_element_type=F32)

        return lax.fori_loop(0, rows_of_one.shape[0] // CHUNK, step, total)

    def cut(mode, rows, send, take, phase):
        group = groups[mode]
        share = extents[mode] // group.size
        for u in range(group.size):
            send[u, 0:share, :] = rows[u * share : (u + 1) * share, :]
            send[u, share : share + counts[mode], :] = marks[mode]
        deal(group, send, take, phase)

    def gather_cut(mode, send, take, phase):
        group = groups[mode]
        share, count = extents[mode] // group.size, counts[mode]
        arrive(group, take, phase)
        take[group.mine] = send[group.mine]
        total = [jnp.zeros((share, rank), F32) for _ in range(count)]
        for u in range(group.size):
            rows = take[u, 0:share, :]
            for g in range(count):
                total[g] = total[g] + rows * take[u, share + g : share + g + 1, :]
        return jnp.concatenate(total, axis=0)

    def settle(mode, send, take, inverse, shares, sums, out, phase):
        group = groups[mode]
        share = extents[mode] // group.size
        solved = dot_high(gather_cut(mode, send, take, phase), inverse)
        shares[group.mine] = solved
        sums[me] = jnp.sum(solved * solved, axis=0, keepdims=True)
        spread(everyone, sums, phase + 1)
        spread(group, shares, phase + 2)
        arrive(everyone, sums, phase + 1)
        squares = jnp.sum(sums[...], axis=0) / lengths[mode]
        scale = lax.rsqrt(squares + EPSILON)
        arrive(group, shares, phase + 2)
        for u in range(group.size):
            rows = shares[u] * scale
            for g in range(counts[mode]):
                start = g * extents[mode] + u * share
                out[start : start + share, :] = rows[g * share : (g + 1) * share, :]

    rows = product(0, block_rows(1, factor_b), block_rows(2, factor_c))
    cut(0, rows, send_0, take_0, 3)
    turn_slices(plane_b, slices_b, whole_b, 0)
    arrive(lines[2], gram_c_buf, 2)
    gram_c = jnp.sum(gram_c_buf[...], axis=0) / lengths[2]
    gram_b = end_slices(whole_b, 0)
    inverse = system_inverse(gram_b, gram_c)
    settle(0, send_0, take_0, inverse, share_0, sums_0, out_a, 3)
    plane_a_buf[p] = gram_of(out_a[...])
    spread(lines[0], plane_a_buf, 6)

    rows = product(1, block_rows(0, out_a), block_rows(2, factor_c))
    cut(1, rows, send_1, take_1, 7)
    arrive(lines[0], plane_a_buf, 6)
    gram_a = jnp.sum(plane_a_buf[...], axis=0) / lengths[0]
    inverse = system_inverse(gram_a, gram_c)
    settle(1, send_1, take_1, inverse, share_1, sums_1, out_b, 7)
    start_slices(gram_of(out_b[...]), plane_2, slices_2, 10)

    rows = product(2, block_rows(0, out_a), block_rows(1, out_b))
    turn_slices(plane_2, slices_2, whole_2, 10)
    cut(2, rows, send_2, take_2, 12)
    gram_b = end_slices(whole_2, 10)
    inverse = system_inverse(gram_a, gram_b)
    settle(2, send_2, take_2, inverse, share_2, sums_2, out_c, 12)

    sent(lines[1], slices_b, 0)
    sent(groups[1], whole_b, 1)
    sent(lines[2], gram_c_buf, 2)
    sent(groups[0], send_0, 3)
    sent(everyone, sums_0, 4)
    sent(groups[0], share_0, 5)
    sent(lines[0], plane_a_buf, 6)
    sent(groups[1], send_1, 7)
    sent(everyone, sums_1, 8)
    sent(groups[1], share_1, 9)
    sent(lines[1], slices_2, 10)
    sent(groups[1], whole_2, 11)
    sent(groups[2], send_2, 12)
    sent(everyone, sums_2, 13)
    sent(groups[2], share_2, 14)


def on_device(sizes, blocks, coords, live, factor_b, factor_c):
    n_i, n_j, n_k = sizes
    n_all = n_i * n_j * n_k
    slots, bi, bj, bk = blocks.shape
    rank = factor_b.shape[1]
    group_sizes = (n_j * n_k, n_i * n_k, n_i * n_j)
    spans = (GI_DEV * bi, factor_b.shape[0], factor_c.shape[0])
    extents = (bi, bj, bk)

    def message(mode):
        rows = extents[mode] // group_sizes[mode] + spans[mode] // extents[mode]
        return (group_sizes[mode], (rows + 7) // 8 * 8, rank)

    def buffer(*shape):
        return pltpu.VMEM(shape, F32)

    slices = [
        buffer(group_sizes[1], rank // group_sizes[1], rank),
        buffer(n_j, rank // group_sizes[1], rank),
        buffer(group_sizes[1], rank // group_sizes[1], rank),
    ]
    vmem = pl.BlockSpec(memory_space=pltpu.VMEM)
    far = pl.BlockSpec(memory_space=pltpu.HBM)
    return pl.pallas_call(
        functools.partial(kernel, sizes),
        out_shape=[jax.ShapeDtypeStruct((span, rank), F32) for span in spans],
        in_specs=[pl.BlockSpec(memory_space=pltpu.SMEM), far, far, far],
        out_specs=[vmem] * 3,
        scratch_shapes=[
            pltpu.VMEM((bi * bj, bk), BF16),
            buffer(*factor_b.shape),
            buffer(*factor_c.shape),
            buffer(bi * bj, bk),
            pltpu.VMEM((bj, bi, bk), BF16),
            buffer(max(bi, bj), rank),
            *slices,
            buffer(n_k, rank, rank),
            buffer(n_i, rank, rank),
            *slices,
            *[buffer(*message(mode)) for mode in range(3)],
            *[buffer(*message(mode)) for mode in range(3)],
            *[buffer(group_sizes[mode], spans[mode] // group_sizes[mode], rank) for mode in range(3)],
            *[buffer(n_all, 1, rank) for mode in range(3)],
            pltpu.SemaphoreType.DMA((3,)),
            pltpu.SemaphoreType.DMA((2, 15)),
        ],
        compiler_params=pltpu.CompilerParams(
            collective_id=0, has_side_effects=True, vmem_limit_bytes=40 * 1024 * 1024
        ),
    )(coords.reshape(coords.shape[0]), blocks.reshape(slots * bi * bj, bk), factor_b, factor_c)


def solution(mesh):
    sizes = (mesh.shape["ia"], mesh.shape["ja"], mesh.shape["ka"])
    placed = (
        P(("ia", "ja", "ka"), None, None, None),
        P(None, ("ia", "ja", "ka")),
        P(("ia", "ja", "ka")),
        P("ja", None),
        P("ka", None),
    )
    return jax.shard_map(
        functools.partial(on_device, sizes),
        mesh=mesh,
        in_specs=placed,
        out_specs=(P("ia", None), P("ja", None), P("ka", None)),
        check_vma=False,
    )
```

time: 73.6 us -> 59.3 us (0.81)
  Pallas kernels: 66.9 us -> 52.7 us
    pallas_call x1, Pallas kernels: 66.9 us -> 52.7 us  [on_device(): pl.pallas_call(functools.partial(kernel, sizes), out_shape=[jax.ShapeDtyp...]
    unnamed x12 -> x11, local copies, waits for them, and re-layouts: 5.83 us -> 5.74 us
where the time goes in v2:
time: 59.3 us; the launch traced here: 59.1 us
  Pallas kernels  52.7 us (89%)
  local copies, waits for them, and re-layouts  5.74 us (10%)
  between operations  0.65 us (1%)
    pallas_call x1, Pallas kernels, on_device(): pl.pallas_call(functools.partial(kernel, sizes), out_shape=[jax.ShapeDtyp...  52.7 us
    unnamed x11, local copies, waits for them, and re-layouts  5.74 us

profile of v2, /device:TPU:0, one launch (start us, length us, event | category | flops | bytes accessed | tf_op | source)
XLA Modules:
  0.0 59.1 jit_solution(2953964460187664150)
XLA Ops:
  0.6 0.0 copy-start.3
  0.6 0.6 %copy-done.3 = s32[3,1]{0,1:T(1,128)S(1)} copy-done((s32[3,1]{0,1:T(1,128)S(1)}, s32[3,1]{0,1:T(1,128)}, u32[]{:S(2)}) %copy-start.3) | copy-done | bytes 36
  1.3 0.0 copy-start
  1.3 1.2 %copy-done = bf16[1,64,64,128]{3,2,1,0:T(8,128)(2,1)S(1)} copy-done((bf16[1,64,64,128]{3,2,1,0:T(8,128)(2,1)S(1)}, bf16[1,64,64,128]{3,2,1,0:T(8,128)(2,1)}, u32[]{:S(2)}) %copy-start) | copy-done | bytes 1048600
  2.5 0.0 copy-start.1
  2.5 0.9 %copy-done.1 = f32[512,128]{1,0:T(8,128)S(1)} copy-done((f32[512,128]{1,0:T(8,128)S(1)}, f32[512,128]{1,0:T(8,128)}, u32[]{:S(2)}) %copy-start.1) | copy-done | bytes 262168
  3.5 0.0 copy-start.2
  3.5 0.9 %copy-done.2 = f32[256,128]{1,0:T(8,128)S(1)} copy-done((f32[256,128]{1,0:T(8,128)S(1)}, f32[256,128]{1,0:T(8,128)}, u32[]{:S(2)}) %copy-start.2) | copy-done | bytes 131096
  4.4 52.7 %shard_map.67 = (f32[256,128]{1,0:T(8,128)S(1)}, f32[256,128]{1,0:T(8,128)S(1)}, f32[512,128]{1,0:T(8,128)S(1)}) custom-call(s32[3]{0:T(128)S(1)} %bitcast.3, bf16[4096,128]{1,0:T(8,128)(2,1)S(1)} %bitcast.2, f32[256,128]{1,0:T(8,128)S(1)} %copy-done.2, f32[512,128]{1,0:T(8,128)S(1)} %copy-done.1), custom_call_target="tpu_custom_call" | custom-call | tf_op jit(solution)/shard_map/pallas_call | solution.py:397
  57.1 0.7 %copy.10 = f32[256,128]{1,0:T(8,128)} copy(f32[256,128]{1,0:T(8,128)S(1)} %get-tuple-element.6) | data formatting | bytes 262144
  57.8 0.7 %copy.11 = f32[256,128]{1,0:T(8,128)} copy(f32[256,128]{1,0:T(8,128)S(1)} %get-tuple-element.7) | data formatting | bytes 262144
  58.4 0.7 %copy.12 = f32[512,128]{1,0:T(8,128)} copy(f32[512,128]{1,0:T(8,128)S(1)} %get-tuple-element.8) | data formatting | bytes 524288
Async XLA Ops:
  0.6 0.7 %copy-start.3 = (s32[3,1]{0,1:T(1,128)S(1)}, s32[3,1]{0,1:T(1,128)}, u32[]{:S(2)}) copy-start(s32[3,1]{0,1:T(1,128)} %param.6) | copy-start | bytes 40
  1.3 1.2 %copy-start = (bf16[1,64,64,128]{3,2,1,0:T(8,128)(2,1)S(1)}, bf16[1,64,64,128]{3,2,1,0:T(8,128)(2,1)}, u32[]{:S(2)}) copy-start(bf16[1,64,64,128]{3,2,1,0:T(8,128)(2,1)} %param.5) | copy-start | bytes 3145732
  2.5 0.9 %copy-start.1 = (f32[512,128]{1,0:T(8,128)S(1)}, f32[512,128]{1,0:T(8,128)}, u32[]{:S(2)}) copy-start(f32[512,128]{1,0:T(8,128)} %factor_c_hbm.1) | copy-start | bytes 786436
  3.5 0.9 %copy-start.2 = (f32[256,128]{1,0:T(8,128)S(1)}, f32[256,128]{1,0:T(8,128)}, u32[]{:S(2)}) copy-start(f32[256,128]{1,0:T(8,128)} %factor_b_hbm.1) | copy-start | bytes 393220

commit v3 on v2

--- a/solution.py
+++ b/solution.py
@@ -63,11 +63,14 @@
     system = merged * unit + (RIDGE_SHARE / order) * eye
     first, scales = newton_plan(order)
     twice = 2.0 * eye
-    guess = (scales[0] * first) * (twice - first * system)
-    for step, scale in enumerate(scales[1:], 1):
-        times = dot_high if step + 2 >= len(scales) else dot_middle
-        residual = twice - times(system, guess)
-        guess = scale * times(guess, residual)
+    start = scales[0] * first
+    guess = start * (twice - first * system)
+    image = start * (2.0 * system - first * dot_middle(system, system))
+    for scale in scales[1:-2]:
+        both = scale * dot_middle(jnp.concatenate([image, guess], axis=0), twice - image)
+        image, guess = both[:order], both[order:]
+    for scale, times in zip(scales[-2:], (dot_middle, dot_high)):
+        guess = scale * times(guess, twice - times(system, guess))
     return guess * unit
 
 
@@ -91,6 +94,7 @@
     factor_c,
     wide,
     turned,
+    upright,
     rows_one,
     plane_b,
     slices_b,
@@ -109,6 +113,7 @@
     share_0,
     share_1,
     share_2,
+    own_sums,
     sums_0,
     sums_1,
     sums_2,
@@ -148,6 +153,27 @@
                 self.size *= sizes[axis]
                 self.mine = self.mine * sizes[axis] + position[axis]
 
+        def outside(self, body):
+            (axis,) = (i for i in range(3) if i not in self.axes)
+
+            def visit(step, index):
+                device, rest, slot = list(position), index, (step - 1) * self.size + self.mine
+                device[axis] = lax.rem(position[axis] + step, sizes[axis])
+                for other in reversed(self.axes):
+                    if isinstance(rest, int):
+                        device[other] = shifted[other][rest % sizes[other]]
+                    else:
+                        device[other] = lax.rem(rest, sizes[other])
+                    rest = rest // sizes[other]
+                body(slot, tuple(device))
+
+            for step in range(1, sizes[axis]):
+                if self.size <= 16:
+                    for index in range(self.size):
+                        visit(step, index)
+                else:
+                    pl.loop(0, self.size)(functools.partial(visit, step))
+
         def partners(self, body):
             if self.size <= 32:
                 for offset in range(1, self.size):
@@ -173,7 +199,6 @@
     everyone = Group(0, 1, 2)
     groups = (Group(1, 2), Group(0, 2), Group(0, 1))
     lines = (Group(0), Group(1), Group(2))
-    me = everyone.mine
 
     def copy(source, target, phase, device):
         return pltpu.make_async_remote_copy(
@@ -273,8 +298,7 @@
             )
             if mode == 2:
                 depth = CHUNK * extents[1]
-                left = tensor[pl.ds(pl.multiple_of(j * depth, depth), depth), :]
-                dims = (((0,), (0,)), ((), ()))
+                left = upright[:, pl.ds(pl.multiple_of(j * depth, depth), depth)]
             else:
                 if mode == 0:
                     parts = [turned[j * CHUNK + i] for i in range(CHUNK)]
@@ -285,10 +309,9 @@
                         for i in range(CHUNK)
                     ]
                 left = jnp.concatenate(parts, axis=1)
-                dims = (((1,), (0,)), ((), ()))
-            return total + lax.dot_general(left, khatri, dims, preferred_element_type=F32)
-
-        return lax.fori_loop(0, rows_of_one.shape[0] // CHUNK, step, total)
+            return total + jnp.dot(left, khatri, preferred_element_type=F32)
+
+        return lax.fori_loop(0, rows_of_one.shape[0] // CHUNK, step, total, unroll=True)
 
     def cut(mode, rows, send, take, phase):
         group = groups[mode]
@@ -310,23 +333,37 @@
                 total[g] = total[g] + rows * take[u, share + g : share + g + 1, :]
         return jnp.concatenate(total, axis=0)
 
-    def settle(mode, send, take, inverse, shares, sums, out, phase):
+    def settle(mode, send, take, inverse, shares, sums, out, phase, meanwhile=None):
         group = groups[mode]
         share = extents[mode] // group.size
         solved = dot_high(gather_cut(mode, send, take, phase), inverse)
         shares[group.mine] = solved
-        sums[me] = jnp.sum(solved * solved, axis=0, keepdims=True)
-        spread(everyone, sums, phase + 1)
         spread(group, shares, phase + 2)
-        arrive(everyone, sums, phase + 1)
-        squares = jnp.sum(sums[...], axis=0) / lengths[mode]
+        own_sums[mode] = jnp.sum(solved * solved, axis=0, keepdims=True)
+        group.outside(
+            lambda slot, device: copy(
+                own_sums.at[mode], sums.at[slot], phase + 1, device
+            ).start()
+        )
+        if meanwhile is not None:
+            meanwhile()
+        copy(sums, sums, phase + 1, position).wait_recv()
+        arrive(group, shares, phase + 2)
+        squares = jnp.sum(sums[...], axis=0)
+        for u in range(group.size):
+            squares = squares + jnp.sum(shares[u] * shares[u], axis=0, keepdims=True)
+        squares = squares / lengths[mode]
         scale = lax.rsqrt(squares + EPSILON)
-        arrive(group, shares, phase + 2)
         for u in range(group.size):
             rows = shares[u] * scale
             for g in range(counts[mode]):
                 start = g * extents[mode] + u * share
                 out[start : start + share, :] = rows[g * share : (g + 1) * share, :]
+
+    def stand_up():
+        depth = CHUNK * extents[1]
+        for start in range(0, tensor.shape[0], depth):
+            upright[:, start : start + depth] = tensor[start : start + depth, :].T
 
     rows = product(0, block_rows(1, factor_b), block_rows(2, factor_c))
     cut(0, rows, send_0, take_0, 3)
@@ -335,7 +372,7 @@
     gram_c = jnp.sum(gram_c_buf[...], axis=0) / lengths[2]
     gram_b = end_slices(whole_b, 0)
     inverse = system_inverse(gram_b, gram_c)
-    settle(0, send_0, take_0, inverse, share_0, sums_0, out_a, 3)
+    settle(0, send_0, take_0, inverse, share_0, sums_0, out_a, 3, stand_up)
     plane_a_buf[p] = gram_of(out_a[...])
     spread(lines[0], plane_a_buf, 6)
 
@@ -358,17 +395,28 @@
     sent(groups[1], whole_b, 1)
     sent(lines[2], gram_c_buf, 2)
     sent(groups[0], send_0, 3)
-    sent(everyone, sums_0, 4)
+    copy(sums_0, sums_0, 4, position).wait_send()
     sent(groups[0], share_0, 5)
     sent(lines[0], plane_a_buf, 6)
     sent(groups[1], send_1, 7)
-    sent(everyone, sums_1, 8)
+    copy(sums_1, sums_1, 8, position).wait_send()
     sent(groups[1], share_1, 9)
     sent(lines[1], slices_2, 10)
     sent(groups[1], whole_2, 11)
     sent(groups[2], send_2, 12)
-    sent(everyone, sums_2, 13)
+    copy(sums_2, sums_2, 13, position).wait_send()
     sent(groups[2], share_2, 14)
+
+
+def store_kernel(one, two, three, out_one, out_two, out_three, sems):
+    copies = [
+        pltpu.make_async_copy(source, target, sems.at[i])
+        for i, (source, target) in enumerate(((one, out_one), (two, out_two), (three, out_three)))
+    ]
+    for copy in copies:
+        copy.start()
+    for copy in copies:
+        copy.wait()
 
 
 def on_device(sizes, blocks, coords, live, factor_b, factor_c):
@@ -394,9 +442,10 @@
     ]
     vmem = pl.BlockSpec(memory_space=pltpu.VMEM)
     far = pl.BlockSpec(memory_space=pltpu.HBM)
-    return pl.pallas_call(
+    shapes = [jax.ShapeDtypeStruct((span, rank), F32) for span in spans]
+    factors = pl.pallas_call(
         functools.partial(kernel, sizes),
-        out_shape=[jax.ShapeDtypeStruct((span, rank), F32) for span in spans],
+        out_shape=shapes,
         in_specs=[pl.BlockSpec(memory_space=pltpu.SMEM), far, far, far],
         out_specs=[vmem] * 3,
         scratch_shapes=[
@@ -405,6 +454,7 @@
             buffer(*factor_c.shape),
             buffer(bi * bj, bk),
             pltpu.VMEM((bj, bi, bk), BF16),
+            pltpu.VMEM((bk, bi * bj), BF16),
             buffer(max(bi, bj), rank),
             *slices,
             buffer(n_k, rank, rank),
@@ -413,14 +463,22 @@
             *[buffer(*message(mode)) for mode in range(3)],
             *[buffer(*message(mode)) for mode in range(3)],
             *[buffer(group_sizes[mode], spans[mode] // group_sizes[mode], rank) for mode in range(3)],
-            *[buffer(n_all, 1, rank) for mode in range(3)],
+            buffer(3, 1, rank),
+            *[buffer(n_all - size, 1, rank) for size in group_sizes],
             pltpu.SemaphoreType.DMA((3,)),
             pltpu.SemaphoreType.DMA((2, 15)),
         ],
         compiler_params=pltpu.CompilerParams(
-            collective_id=0, has_side_effects=True, vmem_limit_bytes=40 * 1024 * 1024
+            collective_id=0, has_side_effects=True, vmem_limit_bytes=48 * 1024 * 1024
         ),
     )(coords.reshape(coords.shape[0]), blocks.reshape(slots * bi * bj, bk), factor_b, factor_c)
+    return pl.pallas_call(
+        store_kernel,
+        out_shape=shapes,
+        in_specs=[pl.BlockSpec(memory_space=pl.ANY)] * 3,
+        out_specs=[far] * 3,
+        scratch_shapes=[pltpu.SemaphoreType.DMA((3,))],
+    )(*factors)
 
 
 def solution(mesh):

time: 59.3 us -> 75.7 us (1.28)
  Pallas kernels: 52.7 us -> 69.1 us
    pallas_call x1 -> x2, Pallas kernels: 52.7 us -> 69.1 us  [the longest x1 52 us: on_device(): pl.pallas_call(functools.partial(kernel, sizes), out_shape=shapes, in_spe...]
    unnamed x11 -> x14, local copies, waits for them, and re-layouts: 5.74 us -> 5.72 us
where the time goes in v3:
time: 75.7 us; the launch traced here: 75.4 us
  Pallas kernels  69.1 us (91%)
  local copies, waits for them, and re-layouts  5.72 us (8%)
    pallas_call x1, Pallas kernels, on_device(): pl.pallas_call(functools.partial(kernel, sizes), out_shape=shapes, in_spe...  52 us
    pallas_call x1, Pallas kernels, on_device(): pl.pallas_call(store_kernel, out_shape=shapes, in_specs=[pl.BlockSpec(mem...  17 us
    unnamed x14, local copies, waits for them, and re-layouts  5.72 us

profile of v3, /device:TPU:0, one launch (start us, length us, event | category | flops | bytes accessed | tf_op | source)
XLA Modules:
  0.0 75.4 jit_solution(71802797371120050)
XLA Ops:
  0.6 0.0 copy-start.6
  0.6 0.6 copy-done.6
  1.3 0.0 copy-start
  1.3 1.2 %copy-done = bf16[1,64,64,128]{3,2,1,0:T(8,128)(2,1)S(1)} copy-done((bf16[1,64,64,128]{3,2,1,0:T(8,128)(2,1)S(1)}, bf16[1,64,64,128]{3,2,1,0:T(8,128)(2,1)}, u32[]{:S(2)}) %copy-start) | copy-done | bytes 1048600
  2.5 0.0 copy-start.2
  2.5 0.9 %copy-done.2 = f32[512,128]{1,0:T(8,128)S(1)} copy-done((f32[512,128]{1,0:T(8,128)S(1)}, f32[512,128]{1,0:T(8,128)}, u32[]{:S(2)}) %copy-start.2) | copy-done | bytes 262168
  3.5 0.0 copy-start.5
  3.5 0.9 %copy-done.5 = f32[256,128]{1,0:T(8,128)S(1)} copy-done((f32[256,128]{1,0:T(8,128)S(1)}, f32[256,128]{1,0:T(8,128)}, u32[]{:S(2)}) %copy-start.5) | copy-done | bytes 131096
  4.4 52.0 %shard_map.67 = (f32[256,128]{1,0:T(8,128)S(1)}, f32[256,128]{1,0:T(8,128)S(1)}, f32[512,128]{1,0:T(8,128)S(1)}) custom-call(s32[3]{0:T(128)S(1)} %bitcast.3, bf16[4096,128]{1,0:T(8,128)(2,1)S(1)} %bitcast.2, f32[256,128]{1,0:T(8,128)S(1)} %copy-done.5, f32[512,128]{1,0:T(8,128)S(1)} %copy-done.2), custom_call_target="tpu_custom_call" | custom-call | tf_op jit(solution)/shard_map/pallas_call | solution.py:446
  56.4 0.0 copy-start.1
  56.4 0.7 copy-done.1
  57.1 0.0 copy-start.3
  57.1 0.6 copy-done.3
  57.8 0.0 copy-start.4
  57.8 0.6 copy-done.4
  58.4 17.0 %shard_map.68 = (f32[256,128]{1,0:T(8,128)}, f32[256,128]{1,0:T(8,128)}, f32[512,128]{1,0:T(8,128)}) custom-call(f32[256,128]{1,0:T(8,128)} %copy-done.3, f32[256,128]{1,0:T(8,128)} %copy-done.4, f32[512,128]{1,0:T(8,128)} %copy-done.1), custom_call_target="tpu_custom_call" | custom-call | tf_op jit(solution)/shard_map/pallas_call | solution.py:475
Async XLA Ops:
  0.6 0.7 copy-start.6
  1.3 1.2 %copy-start = (bf16[1,64,64,128]{3,2,1,0:T(8,128)(2,1)S(1)}, bf16[1,64,64,128]{3,2,1,0:T(8,128)(2,1)}, u32[]{:S(2)}) copy-start(bf16[1,64,64,128]{3,2,1,0:T(8,128)(2,1)} %param.5) | copy-start | bytes 3145732
  2.5 0.9 %copy-start.2 = (f32[512,128]{1,0:T(8,128)S(1)}, f32[512,128]{1,0:T(8,128)}, u32[]{:S(2)}) copy-start(f32[512,128]{1,0:T(8,128)} %factor_c_hbm.1) | copy-start | bytes 786436
  3.5 0.9 %copy-start.5 = (f32[256,128]{1,0:T(8,128)S(1)}, f32[256,128]{1,0:T(8,128)}, u32[]{:S(2)}) copy-start(f32[256,128]{1,0:T(8,128)} %factor_b_hbm.1) | copy-start | bytes 393220
  56.4 0.7 copy-start.1
  57.1 0.7 copy-start.3
  57.8 0.7 copy-start.4

commit v4 on v3

--- a/solution.py
+++ b/solution.py
@@ -66,11 +66,10 @@
     start = scales[0] * first
     guess = start * (twice - first * system)
     image = start * (2.0 * system - first * dot_middle(system, system))
-    for scale in scales[1:-2]:
+    for scale in scales[1:-1]:
         both = scale * dot_middle(jnp.concatenate([image, guess], axis=0), twice - image)
         image, guess = both[:order], both[order:]
-    for scale, times in zip(scales[-2:], (dot_middle, dot_high)):
-        guess = scale * times(guess, twice - times(system, guess))
+    guess = scales[-1] * dot_high(guess, twice - dot_high(system, guess))
     return guess * unit
 
 
@@ -119,6 +118,7 @@
     sums_2,
     load_sems,
     sems,
+    line_sems,
 ):
     n_i, n_j, n_k = sizes
     n_all = n_i * n_j * n_k
@@ -333,12 +333,42 @@
                 total[g] = total[g] + rows * take[u, share + g : share + g + 1, :]
         return jnp.concatenate(total, axis=0)
 
-    def settle(mode, send, take, inverse, shares, sums, out, phase, meanwhile=None):
+    def line_copy(group, buffer, step, column):
+        slot = buffer.at[p * n_j + column]
+        return pltpu.make_async_remote_copy(
+            src_ref=slot,
+            dst_ref=slot,
+            send_sem=line_sems.at[0, step],
+            recv_sem=line_sems.at[1, step],
+            device_id=(p, shifted[1][step], s),
+            device_id_type=MESH,
+        )
+
+    def start_relay(group, buffer, phase):
+        for step in range(1, n_j):
+            line_copy(group, buffer, step, q).start()
+        slot = buffer.at[group.mine]
+        lines[0].partners(lambda other, device: copy(slot, slot, phase, device).start())
+
+    def end_relay(group, buffer, phase):
+        for step in range(1, n_j):
+            column = shifted[1][n_j - step]
+            line_copy(group, buffer, step, column).wait_recv()
+            slot = buffer.at[p * n_j + column]
+            lines[0].partners(
+                lambda other, device, slot=slot: copy(slot, slot, phase, device).start()
+            )
+        copy(*[buffer.at[pl.ds(0, (n_i - 1) * n_j)]] * 2, phase, position).wait_recv()
+
+    def settle(mode, send, take, inverse, shares, sums, out, phase, meanwhile=None, relay=False):
         group = groups[mode]
         share = extents[mode] // group.size
         solved = dot_high(gather_cut(mode, send, take, phase), inverse)
         shares[group.mine] = solved
-        spread(group, shares, phase + 2)
+        if relay:
+            start_relay(group, shares, phase + 2)
+        else:
+            spread(group, shares, phase + 2)
         own_sums[mode] = jnp.sum(solved * solved, axis=0, keepdims=True)
         group.outside(
             lambda slot, device: copy(
@@ -347,8 +377,11 @@
         )
         if meanwhile is not None:
             meanwhile()
+        if relay:
+            end_relay(group, shares, phase + 2)
+        else:
+            arrive(group, shares, phase + 2)
         copy(sums, sums, phase + 1, position).wait_recv()
-        arrive(group, shares, phase + 2)
         squares = jnp.sum(sums[...], axis=0)
         for u in range(group.size):
             squares = squares + jnp.sum(shares[u] * shares[u], axis=0, keepdims=True)
@@ -389,7 +422,7 @@
     cut(2, rows, send_2, take_2, 12)
     gram_b = end_slices(whole_2, 10)
     inverse = system_inverse(gram_a, gram_b)
-    settle(2, send_2, take_2, inverse, share_2, sums_2, out_c, 12)
+    settle(2, send_2, take_2, inverse, share_2, sums_2, out_c, 12, relay=True)
 
     sent(lines[1], slices_b, 0)
     sent(groups[1], whole_b, 1)
@@ -405,18 +438,9 @@
     sent(groups[1], whole_2, 11)
     sent(groups[2], send_2, 12)
     copy(sums_2, sums_2, 13, position).wait_send()
-    sent(groups[2], share_2, 14)
-
-
-def store_kernel(one, two, three, out_one, out_two, out_three, sems):
-    copies = [
-        pltpu.make_async_copy(source, target, sems.at[i])
-        for i, (source, target) in enumerate(((one, out_one), (two, out_two), (three, out_three)))
-    ]
-    for copy in copies:
-        copy.start()
-    for copy in copies:
-        copy.wait()
+    for step in range(1, n_j):
+        line_copy(groups[2], share_2, step, q).wait_send()
+    copy(*[share_2.at[pl.ds(0, (n_i - 1) * n_j)]] * 2, 14, position).wait_send()
 
 
 def on_device(sizes, blocks, coords, live, factor_b, factor_c):
@@ -443,7 +467,7 @@
     vmem = pl.BlockSpec(memory_space=pltpu.VMEM)
     far = pl.BlockSpec(memory_space=pltpu.HBM)
     shapes = [jax.ShapeDtypeStruct((span, rank), F32) for span in spans]
-    factors = pl.pallas_call(
+    return pl.pallas_call(
         functools.partial(kernel, sizes),
         out_shape=shapes,
         in_specs=[pl.BlockSpec(memory_space=pltpu.SMEM), far, far, far],
@@ -467,18 +491,18 @@
             *[buffer(n_all - size, 1, rank) for size in group_sizes],
             pltpu.SemaphoreType.DMA((3,)),
             pltpu.SemaphoreType.DMA((2, 15)),
+            pltpu.SemaphoreType.DMA((2, n_j)),
         ],
         compiler_params=pltpu.CompilerParams(
             collective_id=0, has_side_effects=True, vmem_limit_bytes=48 * 1024 * 1024
         ),
-    )(coords.reshape(coords.shape[0]), blocks.reshape(slots * bi * bj, bk), factor_b, factor_c)
-    return pl.pallas_call(
-        store_kernel,
-        out_shape=shapes,
-        in_specs=[pl.BlockSpec(memory_space=pl.ANY)] * 3,
-        out_specs=[far] * 3,
-        scratch_shapes=[pltpu.SemaphoreType.DMA((3,))],
-    )(*factors)
+    )(
+        coords.reshape(coords.shape[0]),
+        *(
+            pltpu.with_memory_space_constraint(array, pltpu.HBM)
+            for array in (blocks.reshape(slots * bi * bj, bk), factor_b, factor_c)
+        ),
+    )
 
 
 def solution(mesh):

time: 75.7 us -> 54.3 us (0.72)
  Pallas kernels: 69.1 us -> 50.8 us
  local copies, waits for them, and re-layouts: 5.72 us -> 2.66 us
    pallas_call x1 -> x0, Pallas kernels: 17 us -> none  [on_device(): pl.pallas_call(store_kernel, out_shape=shapes, in_specs=[pl.BlockSpec(mem...]
    unnamed x14 -> x5, local copies, waits for them, and re-layouts: 5.72 us -> 2.66 us
    pallas_call x1, Pallas kernels: 52 us -> 50.8 us  [on_device(): pl.pallas_call(functools.partial(kernel, sizes), out_shape=shapes, in_spe...]
where the time goes in v4:
time: 54.3 us; the launch traced here: 54.1 us
  Pallas kernels  50.8 us (94%)
  local copies, waits for them, and re-layouts  2.66 us (5%)
  between operations  0.65 us (1%)
    pallas_call x1, Pallas kernels, on_device(): pl.pallas_call(functools.partial(kernel, sizes), out_shape=shapes, in_spe...  50.8 us
    unnamed x5, local copies, waits for them, and re-layouts  2.66 us

profile of v4, /device:TPU:0, one launch (start us, length us, event | category | flops | bytes accessed | tf_op | source)
XLA Modules:
  0.0 54.1 jit_solution(16313329431178344871)
XLA Ops:
  0.6 0.0 copy-start
  0.6 0.6 %copy-done = s32[3,1]{0,1:T(1,128)S(1)} copy-done((s32[3,1]{0,1:T(1,128)S(1)}, s32[3,1]{0,1:T(1,128)}, u32[]{:S(2)}) %copy-start) | copy-done | bytes 36
  1.3 50.8 %shard_map.67 = (f32[256,128]{1,0:T(8,128)S(1)}, f32[256,128]{1,0:T(8,128)S(1)}, f32[512,128]{1,0:T(8,128)S(1)}) custom-call(s32[3]{0:T(128)S(1)} %bitcast.2, bf16[4096,128]{1,0:T(8,128)(2,1)} %bitcast.3, f32[256,128]{1,0:T(8,128)} %factor_b_hbm.1, f32[512,128]{1,0:T(8,128)} %factor_c_hbm.1), custom_call_target="tpu_custom_call" | custom-call | tf_op jit(solution)/shard_map/pallas_call | solution.py:470
  52.1 0.7 %copy.10 = f32[256,128]{1,0:T(8,128)} copy(f32[256,128]{1,0:T(8,128)S(1)} %get-tuple-element.6) | data formatting | bytes 262144
  52.8 0.7 %copy.11 = f32[256,128]{1,0:T(8,128)} copy(f32[256,128]{1,0:T(8,128)S(1)} %get-tuple-element.7) | data formatting | bytes 262144
  53.4 0.7 %copy.12 = f32[512,128]{1,0:T(8,128)} copy(f32[512,128]{1,0:T(8,128)S(1)} %get-tuple-element.8) | data formatting | bytes 524288
Async XLA Ops:
  0.6 0.7 %copy-start = (s32[3,1]{0,1:T(1,128)S(1)}, s32[3,1]{0,1:T(1,128)}, u32[]{:S(2)}) copy-start(s32[3,1]{0,1:T(1,128)} %param.6) | copy-start | bytes 40

commit v5 on v4

--- a/solution.py
+++ b/solution.py
@@ -112,7 +112,6 @@
     share_0,
     share_1,
     share_2,
-    own_sums,
     sums_0,
     sums_1,
     sums_2,
@@ -152,27 +151,6 @@
             for axis in axes:
                 self.size *= sizes[axis]
                 self.mine = self.mine * sizes[axis] + position[axis]
-
-        def outside(self, body):
-            (axis,) = (i for i in range(3) if i not in self.axes)
-
-            def visit(step, index):
-                device, rest, slot = list(position), index, (step - 1) * self.size + self.mine
-                device[axis] = lax.rem(position[axis] + step, sizes[axis])
-                for other in reversed(self.axes):
-                    if isinstance(rest, int):
-                        device[other] = shifted[other][rest % sizes[other]]
-                    else:
-                        device[other] = lax.rem(rest, sizes[other])
-                    rest = rest // sizes[other]
-                body(slot, tuple(device))
-
-            for step in range(1, sizes[axis]):
-                if self.size <= 16:
-                    for index in range(self.size):
-                        visit(step, index)
-                else:
-                    pl.loop(0, self.size)(functools.partial(visit, step))
 
         def partners(self, body):
             if self.size <= 32:
@@ -360,87 +338,113 @@
             )
         copy(*[buffer.at[pl.ds(0, (n_i - 1) * n_j)]] * 2, phase, position).wait_recv()
 
-    def settle(mode, send, take, inverse, shares, sums, out, phase, meanwhile=None, relay=False):
+    def settle(mode, send, take, shares, sums, out, phase, inverse_of, gram_away, relay=False):
         group = groups[mode]
         share = extents[mode] // group.size
-        solved = dot_high(gather_cut(mode, send, take, phase), inverse)
-        shares[group.mine] = solved
+        shares[group.mine] = gather_cut(mode, send, take, phase)
         if relay:
             start_relay(group, shares, phase + 2)
         else:
             spread(group, shares, phase + 2)
-        own_sums[mode] = jnp.sum(solved * solved, axis=0, keepdims=True)
-        group.outside(
-            lambda slot, device: copy(
-                own_sums.at[mode], sums.at[slot], phase + 1, device
-            ).start()
-        )
-        if meanwhile is not None:
-            meanwhile()
+        inverse = inverse_of()
         if relay:
             end_relay(group, shares, phase + 2)
         else:
             arrive(group, shares, phase + 2)
-        copy(sums, sums, phase + 1, position).wait_recv()
-        squares = jnp.sum(sums[...], axis=0)
+        solved = dot_high(shares[...].reshape(spans[mode], rank), inverse)
+        sums[lines[mode].mine] = jnp.sum(solved * solved, axis=0, keepdims=True)
+        spread(lines[mode], sums, phase + 1)
+        gram_away(solved)
+        arrive(lines[mode], sums, phase + 1)
+        scale = lax.rsqrt(jnp.sum(sums[...], axis=0) / lengths[mode] + EPSILON)
+        scaled = solved * scale
         for u in range(group.size):
-            squares = squares + jnp.sum(shares[u] * shares[u], axis=0, keepdims=True)
-        squares = squares / lengths[mode]
-        scale = lax.rsqrt(squares + EPSILON)
-        for u in range(group.size):
-            rows = shares[u] * scale
             for g in range(counts[mode]):
                 start = g * extents[mode] + u * share
-                out[start : start + share, :] = rows[g * share : (g + 1) * share, :]
+                source = (u * counts[mode] + g) * share
+                out[start : start + share, :] = scaled[source : source + share, :]
+        return scale
+
+    def scaled_gram(gram, scale):
+        return gram * jnp.broadcast_to(scale, (rank, rank)).T * scale
 
     def stand_up():
         depth = CHUNK * extents[1]
         for start in range(0, tensor.shape[0], depth):
             upright[:, start : start + depth] = tensor[start : start + depth, :].T
 
+    turn_slices(plane_b, slices_b, whole_b, 0)
     rows = product(0, block_rows(1, factor_b), block_rows(2, factor_c))
     cut(0, rows, send_0, take_0, 3)
-    turn_slices(plane_b, slices_b, whole_b, 0)
-    arrive(lines[2], gram_c_buf, 2)
-    gram_c = jnp.sum(gram_c_buf[...], axis=0) / lengths[2]
-    gram_b = end_slices(whole_b, 0)
-    inverse = system_inverse(gram_b, gram_c)
-    settle(0, send_0, take_0, inverse, share_0, sums_0, out_a, 3, stand_up)
-    plane_a_buf[p] = gram_of(out_a[...])
-    spread(lines[0], plane_a_buf, 6)
+    stand_up()
+    first = {}
+
+    def inverse_0():
+        arrive(lines[2], gram_c_buf, 2)
+        first["c"] = jnp.sum(gram_c_buf[...], axis=0) / lengths[2]
+        return system_inverse(end_slices(whole_b, 0), first["c"])
+
+    def gram_away_0(solved):
+        plane_a_buf[p] = gram_of(solved)
+        spread(lines[0], plane_a_buf, 6)
+
+    scale_a = settle(0, send_0, take_0, share_0, sums_0, out_a, 3, inverse_0, gram_away_0)
+    gram_c = first["c"]
 
     rows = product(1, block_rows(0, out_a), block_rows(2, factor_c))
     cut(1, rows, send_1, take_1, 7)
-    arrive(lines[0], plane_a_buf, 6)
-    gram_a = jnp.sum(plane_a_buf[...], axis=0) / lengths[0]
-    inverse = system_inverse(gram_a, gram_c)
-    settle(1, send_1, take_1, inverse, share_1, sums_1, out_b, 7)
-    start_slices(gram_of(out_b[...]), plane_2, slices_2, 10)
+
+    def inverse_1():
+        arrive(lines[0], plane_a_buf, 6)
+        total = jnp.sum(plane_a_buf[...], axis=0) / lengths[0]
+        first["a"] = scaled_gram(total, scale_a)
+        return system_inverse(first["a"], gram_c)
+
+    def gram_away_1(solved):
+        start_slices(gram_of(solved), plane_2, slices_2, 10)
+
+    scale_b = settle(1, send_1, take_1, share_1, sums_1, out_b, 7, inverse_1, gram_away_1)
+    gram_a = first["a"]
 
     rows = product(2, block_rows(0, out_a), block_rows(1, out_b))
+    cut(2, rows, send_2, take_2, 12)
     turn_slices(plane_2, slices_2, whole_2, 10)
-    cut(2, rows, send_2, take_2, 12)
-    gram_b = end_slices(whole_2, 10)
-    inverse = system_inverse(gram_a, gram_b)
-    settle(2, send_2, take_2, inverse, share_2, sums_2, out_c, 12, relay=True)
+
+    def inverse_2():
+        return system_inverse(gram_a, scaled_gram(end_slices(whole_2, 10), scale_b))
+
+    settle(
+        2, send_2, take_2, share_2, sums_2, out_c, 12, inverse_2, lambda solved: None, relay=True
+    )
 
     sent(lines[1], slices_b, 0)
     sent(groups[1], whole_b, 1)
     sent(lines[2], gram_c_buf, 2)
     sent(groups[0], send_0, 3)
-    copy(sums_0, sums_0, 4, position).wait_send()
+    sent(lines[0], sums_0, 4)
     sent(groups[0], share_0, 5)
     sent(lines[0], plane_a_buf, 6)
     sent(groups[1], send_1, 7)
-    copy(sums_1, sums_1, 8, position).wait_send()
+    sent(lines[1], sums_1, 8)
     sent(groups[1], share_1, 9)
     sent(lines[1], slices_2, 10)
     sent(groups[1], whole_2, 11)
     sent(groups[2], send_2, 12)
-    copy(sums_2, sums_2, 13, position).wait_send()
+    sent(lines[2], sums_2, 13)
     for step in range(1, n_j):
         line_copy(groups[2], share_2, step, q).wait_send()
     copy(*[share_2.at[pl.ds(0, (n_i - 1) * n_j)]] * 2, 14, position).wait_send()
+
+
+def store_kernel(one, two, three, out_one, out_two, out_three, sems):
+    copies = [
+        pltpu.make_async_copy(source, target, sems.at[i])
+        for i, (source, target) in enumerate(((one, out_one), (two, out_two), (three, out_three)))
+    ]
+    for copy in copies:
+        copy.start()
+    for copy in copies:
+        copy.wait()
 
 
 def on_device(sizes, blocks, coords, live, factor_b, factor_c):
@@ -467,7 +471,7 @@
     vmem = pl.BlockSpec(memory_space=pltpu.VMEM)
     far = pl.BlockSpec(memory_space=pltpu.HBM)
     shapes = [jax.ShapeDtypeStruct((span, rank), F32) for span in spans]
-    return pl.pallas_call(
+    factors = pl.pallas_call(
         functools.partial(kernel, sizes),
         out_shape=shapes,
         in_specs=[pl.BlockSpec(memory_space=pltpu.SMEM), far, far, far],
@@ -487,8 +491,7 @@
             *[buffer(*message(mode)) for mode in range(3)],
             *[buffer(*message(mode)) for mode in range(3)],
             *[buffer(group_sizes[mode], spans[mode] // group_sizes[mode], rank) for mode in range(3)],
-            buffer(3, 1, rank),
-            *[buffer(n_all - size, 1, rank) for size in group_sizes],
+            *[buffer(size, 1, rank) for size in sizes],
             pltpu.SemaphoreType.DMA((3,)),
             pltpu.SemaphoreType.DMA((2, 15)),
             pltpu.SemaphoreType.DMA((2, n_j)),
@@ -503,6 +506,13 @@
             for array in (blocks.reshape(slots * bi * bj, bk), factor_b, factor_c)
         ),
     )
+    return pl.pallas_call(
+        store_kernel,
+        out_shape=[jax.ShapeDtypeStruct((span, rank), F32) for span in spans],
+        in_specs=[vmem] * 3,
+        out_specs=[far] * 3,
+        scratch_shapes=[pltpu.SemaphoreType.DMA((3,))],
+    )(*factors)
 
 
 def solution(mesh):

time: 54.3 us -> 56.2 us (1.035)
  Pallas kernels: 50.8 us -> 52.7 us
    pallas_call x0 -> x1, Pallas kernels: none -> 1.9 us  [on_device(): pl.pallas_call(store_kernel, out_shape=[jax.ShapeDtypeStruct((span, rank)...]
    unnamed x5 -> x8, local copies, waits for them, and re-layouts: 2.66 us -> 2.64 us
where the time goes in v5:
time: 56.2 us; the launch traced here: 56 us
  Pallas kernels  52.7 us (94%)
  local copies, waits for them, and re-layouts  2.64 us (5%)
  between operations  0.66 us (1%)
    pallas_call x1, Pallas kernels, on_device(): pl.pallas_call(functools.partial(kernel, sizes), out_shape=shapes, in_spe...  50.8 us
    unnamed x8, local copies, waits for them, and re-layouts  2.64 us
    pallas_call x1, Pallas kernels, on_device(): pl.pallas_call(store_kernel, out_shape=[jax.ShapeDtypeStruct((span, rank)...  1.9 us

profile of v5, /device:TPU:0, one launch (start us, length us, event | category | flops | bytes accessed | tf_op | source)
XLA Modules:
  0.0 56.0 jit_solution(6098905703471301313)
XLA Ops:
  0.6 0.0 copy-start.3
  0.6 0.6 %copy-done.3 = s32[3,1]{0,1:T(1,128)S(1)} copy-done((s32[3,1]{0,1:T(1,128)S(1)}, s32[3,1]{0,1:T(1,128)}, u32[]{:S(2)}) %copy-start.3) | copy-done | bytes 36
  1.3 50.8 %shard_map.67 = (f32[256,128]{1,0:T(8,128)S(1)}, f32[256,128]{1,0:T(8,128)S(1)}, f32[512,128]{1,0:T(8,128)S(1)}) custom-call(s32[3]{0:T(128)S(1)} %bitcast.2, bf16[4096,128]{1,0:T(8,128)(2,1)} %bitcast.3, f32[256,128]{1,0:T(8,128)} %factor_b_hbm.1, f32[512,128]{1,0:T(8,128)} %factor_c_hbm.1), custom_call_target="tpu_custom_call" | custom-call | tf_op jit(solution)/shard_map/pallas_call | solution.py:474
  52.1 0.0 copy-start
  52.1 0.7 %copy-done = f32[512,128]{1,0:T(8,128)} copy-done((f32[512,128]{1,0:T(8,128)}, f32[512,128]{1,0:T(8,128)S(1)}, u32[]{:S(2)}) %copy-start) | copy-done | bytes 262168
  52.8 0.0 copy-start.1
  52.8 0.6 %copy-done.1 = f32[256,128]{1,0:T(8,128)} copy-done((f32[256,128]{1,0:T(8,128)}, f32[256,128]{1,0:T(8,128)S(1)}, u32[]{:S(2)}) %copy-start.1) | copy-done | bytes 131096
  53.5 0.0 copy-start.2
  53.5 0.7 %copy-done.2 = f32[256,128]{1,0:T(8,128)} copy-done((f32[256,128]{1,0:T(8,128)}, f32[256,128]{1,0:T(8,128)S(1)}, u32[]{:S(2)}) %copy-start.2) | copy-done | bytes 131096
  54.1 1.9 %shard_map.68 = (f32[256,128]{1,0:T(8,128)}, f32[256,128]{1,0:T(8,128)}, f32[512,128]{1,0:T(8,128)}) custom-call(f32[256,128]{1,0:T(8,128)} %copy-done.1, f32[256,128]{1,0:T(8,128)} %copy-done.2, f32[512,128]{1,0:T(8,128)} %copy-done), custom_call_target="tpu_custom_call" | custom-call | tf_op jit(solution)/shard_map/pallas_call | solution.py:509
Async XLA Ops:
  0.6 0.7 %copy-start.3 = (s32[3,1]{0,1:T(1,128)S(1)}, s32[3,1]{0,1:T(1,128)}, u32[]{:S(2)}) copy-start(s32[3,1]{0,1:T(1,128)} %param.6) | copy-start | bytes 40
  52.1 0.7 %copy-start = (f32[512,128]{1,0:T(8,128)}, f32[512,128]{1,0:T(8,128)S(1)}, u32[]{:S(2)}) copy-start(f32[512,128]{1,0:T(8,128)S(1)} %get-tuple-element.8.three) | copy-start | bytes 786436
  52.8 0.6 %copy-start.1 = (f32[256,128]{1,0:T(8,128)}, f32[256,128]{1,0:T(8,128)S(1)}, u32[]{:S(2)}) copy-start(f32[256,128]{1,0:T(8,128)S(1)} %get-tuple-element.6.one) | copy-start | bytes 393220
  53.5 0.7 %copy-start.2 = (f32[256,128]{1,0:T(8,128)}, f32[256,128]{1,0:T(8,128)S(1)}, u32[]{:S(2)}) copy-start(f32[256,128]{1,0:T(8,128)S(1)} %get-tuple-element.7.two) | copy-start | bytes 393220

commit v6 on v4

--- a/solution.py
+++ b/solution.py
@@ -104,13 +104,11 @@
     slices_2,
     whole_2,
     send_0,
-    send_1,
     send_2,
     take_0,
-    take_1,
     take_2,
     share_0,
-    share_1,
+    all_1,
     share_2,
     own_sums,
     sums_0,
@@ -398,9 +396,12 @@
         for start in range(0, tensor.shape[0], depth):
             upright[:, start : start + depth] = tensor[start : start + depth, :].T
 
+    def scaled_gram(gram, scale):
+        return gram * jnp.broadcast_to(scale, (rank, rank)).T * scale
+
+    turn_slices(plane_b, slices_b, whole_b, 0)
     rows = product(0, block_rows(1, factor_b), block_rows(2, factor_c))
     cut(0, rows, send_0, take_0, 3)
-    turn_slices(plane_b, slices_b, whole_b, 0)
     arrive(lines[2], gram_c_buf, 2)
     gram_c = jnp.sum(gram_c_buf[...], axis=0) / lengths[2]
     gram_b = end_slices(whole_b, 0)
@@ -410,17 +411,36 @@
     spread(lines[0], plane_a_buf, 6)
 
     rows = product(1, block_rows(0, out_a), block_rows(2, factor_c))
-    cut(1, rows, send_1, take_1, 7)
+    height, mine = extents[1], groups[1].mine
+    all_1[mine, 0:height, :] = rows
+    all_1[mine, height : height + counts[1], :] = marks[1]
+    spread(groups[1], all_1, 7)
     arrive(lines[0], plane_a_buf, 6)
     gram_a = jnp.sum(plane_a_buf[...], axis=0) / lengths[0]
     inverse = system_inverse(gram_a, gram_c)
-    settle(1, send_1, take_1, inverse, share_1, sums_1, out_b, 7)
-    start_slices(gram_of(out_b[...]), plane_2, slices_2, 10)
-
+    arrive(groups[1], all_1, 7)
+    summed = jnp.concatenate(
+        [
+            sum(
+                all_1[u, 0:height, :] * all_1[u, height + g : height + g + 1, :]
+                for u in range(groups[1].size)
+            )
+            for g in range(counts[1])
+        ],
+        axis=0,
+    )
+    solved = dot_high(summed, inverse)
+    sums_1[q] = jnp.sum(solved * solved, axis=0, keepdims=True)
+    spread(lines[1], sums_1, 8)
+    start_slices(gram_of(solved), plane_2, slices_2, 10)
+    arrive(lines[1], sums_1, 8)
+    scale_b = lax.rsqrt(jnp.sum(sums_1[...], axis=0) / lengths[1] + EPSILON)
+    out_b[...] = solved * scale_b
+
+    turn_slices(plane_2, slices_2, whole_2, 10)
     rows = product(2, block_rows(0, out_a), block_rows(1, out_b))
-    turn_slices(plane_2, slices_2, whole_2, 10)
     cut(2, rows, send_2, take_2, 12)
-    gram_b = end_slices(whole_2, 10)
+    gram_b = scaled_gram(end_slices(whole_2, 10), scale_b)
     inverse = system_inverse(gram_a, gram_b)
     settle(2, send_2, take_2, inverse, share_2, sums_2, out_c, 12, relay=True)
 
@@ -431,9 +451,8 @@
     copy(sums_0, sums_0, 4, position).wait_send()
     sent(groups[0], share_0, 5)
     sent(lines[0], plane_a_buf, 6)
-    sent(groups[1], send_1, 7)
-    copy(sums_1, sums_1, 8, position).wait_send()
-    sent(groups[1], share_1, 9)
+    sent(groups[1], all_1, 7)
+    sent(lines[1], sums_1, 8)
     sent(lines[1], slices_2, 10)
     sent(groups[1], whole_2, 11)
     sent(groups[2], send_2, 12)
@@ -484,11 +503,15 @@
             buffer(n_k, rank, rank),
             buffer(n_i, rank, rank),
             *slices,
-            *[buffer(*message(mode)) for mode in range(3)],
-            *[buffer(*message(mode)) for mode in range(3)],
-            *[buffer(group_sizes[mode], spans[mode] // group_sizes[mode], rank) for mode in range(3)],
+            *[buffer(*message(mode)) for mode in (0, 2)],
+            *[buffer(*message(mode)) for mode in (0, 2)],
+            buffer(group_sizes[0], spans[0] // group_sizes[0], rank),
+            buffer(group_sizes[1], bj + (spans[1] // bj + 7) // 8 * 8, rank),
+            buffer(group_sizes[2], spans[2] // group_sizes[2], rank),
             buffer(3, 1, rank),
-            *[buffer(n_all - size, 1, rank) for size in group_sizes],
+            buffer(n_all - group_sizes[0], 1, rank),
+            buffer(n_j, 1, rank),
+            buffer(n_all - group_sizes[2], 1, rank),
             pltpu.SemaphoreType.DMA((3,)),
             pltpu.SemaphoreType.DMA((2, 15)),
             pltpu.SemaphoreType.DMA((2, n_j)),

time: 54.3 us -> 51.4 us (0.947)
  Pallas kernels: 50.8 us -> 48 us
    pallas_call x1, Pallas kernels: 50.8 us -> 48 us  [on_device(): pl.pallas_call(functools.partial(kernel, sizes), out_shape=shapes, in_spe...]
where the time goes in v6:
time: 51.4 us; the launch traced here: 51.3 us
  Pallas kernels  48 us (93%)
  local copies, waits for them, and re-layouts  2.66 us (5%)
  between operations  0.65 us (1%)
    pallas_call x1, Pallas kernels, on_device(): pl.pallas_call(functools.partial(kernel, sizes), out_shape=shapes, in_spe...  48 us
    unnamed x5, local copies, waits for them, and re-layouts  2.66 us

profile of v6, /device:TPU:0, one launch (start us, length us, event | category | flops | bytes accessed | tf_op | source)
XLA Modules:
  0.0 51.3 jit_solution(14931258424696095279)
XLA Ops:
  0.6 0.0 copy-start
  0.6 0.6 %copy-done = s32[3,1]{0,1:T(1,128)S(1)} copy-done((s32[3,1]{0,1:T(1,128)S(1)}, s32[3,1]{0,1:T(1,128)}, u32[]{:S(2)}) %copy-start) | copy-done | bytes 36
  1.3 48.0 %shard_map.67 = (f32[256,128]{1,0:T(8,128)S(1)}, f32[256,128]{1,0:T(8,128)S(1)}, f32[512,128]{1,0:T(8,128)S(1)}) custom-call(s32[3]{0:T(128)S(1)} %bitcast.2, bf16[4096,128]{1,0:T(8,128)(2,1)} %bitcast.3, f32[256,128]{1,0:T(8,128)} %factor_b_hbm.1, f32[512,128]{1,0:T(8,128)} %factor_c_hbm.1), custom_call_target="tpu_custom_call" | custom-call | tf_op jit(solution)/shard_map/pallas_call | solution.py:489
  49.3 0.7 %copy.10 = f32[256,128]{1,0:T(8,128)} copy(f32[256,128]{1,0:T(8,128)S(1)} %get-tuple-element.6) | data formatting | bytes 262144
  49.9 0.7 %copy.11 = f32[256,128]{1,0:T(8,128)} copy(f32[256,128]{1,0:T(8,128)S(1)} %get-tuple-element.7) | data formatting | bytes 262144
  50.6 0.7 %copy.12 = f32[512,128]{1,0:T(8,128)} copy(f32[512,128]{1,0:T(8,128)S(1)} %get-tuple-element.8) | data formatting | bytes 524288
Async XLA Ops:
  0.6 0.7 %copy-start = (s32[3,1]{0,1:T(1,128)S(1)}, s32[3,1]{0,1:T(1,128)}, u32[]{:S(2)}) copy-start(s32[3,1]{0,1:T(1,128)} %param.6) | copy-start | bytes 40

commit v7 on v6

--- a/solution.py
+++ b/solution.py
@@ -81,13 +81,14 @@
 
 def kernel(
     sizes,
-    coords,
+    coords_hbm,
     tensor_hbm,
     factor_b_hbm,
     factor_c_hbm,
     out_a,
     out_b,
     out_c,
+    coords,
     tensor,
     factor_b,
     factor_c,
@@ -130,7 +131,7 @@
     loads = [
         pltpu.make_async_copy(source, target, load_sems.at[i])
         for i, (source, target) in enumerate(
-            ((factor_b_hbm, factor_b), (factor_c_hbm, factor_c), (tensor_hbm, tensor))
+            ((factor_b_hbm, factor_b), (factor_c_hbm, factor_c), (tensor_hbm, tensor), (coords_hbm, coords))
         )
     ]
     for load in loads:
@@ -261,6 +262,9 @@
     first_gram_b = gram_of(factor_b[...])
     loads[1].wait()
     gram_c_buf[s] = gram_of(factor_c[...])
+    loads[2].wait()
+    wide[...] = tensor[...].astype(F32)
+    loads[3].wait()
     pl.semaphore_wait(barrier, n_all - 1)
     start_slices(first_gram_b, plane_b, slices_b, 0)
     spread(lines[2], gram_c_buf, 2)
@@ -277,9 +281,6 @@
             source[g * extent : (g + 1) * extent, :] * marks[mode][g : g + 1, :]
             for g in range(counts[mode])
         )
-
-    loads[2].wait()
-    wide[...] = tensor[...].astype(F32)
 
     @pl.loop(0, extents[1], unroll=8)
     def _(b):
@@ -489,9 +490,10 @@
     return pl.pallas_call(
         functools.partial(kernel, sizes),
         out_shape=shapes,
-        in_specs=[pl.BlockSpec(memory_space=pltpu.SMEM), far, far, far],
+        in_specs=[far, far, far, far],
         out_specs=[vmem] * 3,
         scratch_shapes=[
+            pltpu.SMEM((coords.shape[0],), jnp.int32),
             pltpu.VMEM((bi * bj, bk), BF16),
             buffer(*factor_b.shape),
             buffer(*factor_c.shape),
@@ -512,7 +514,7 @@
             buffer(n_all - group_sizes[0], 1, rank),
             buffer(n_j, 1, rank),
             buffer(n_all - group_sizes[2], 1, rank),
-            pltpu.SemaphoreType.DMA((3,)),
+            pltpu.SemaphoreType.DMA((4,)),
             pltpu.SemaphoreType.DMA((2, 15)),
             pltpu.SemaphoreType.DMA((2, n_j)),
         ],
@@ -520,10 +522,9 @@
             collective_id=0, has_side_effects=True, vmem_limit_bytes=48 * 1024 * 1024
         ),
     )(
-        coords.reshape(coords.shape[0]),
         *(
             pltpu.with_memory_space_constraint(array, pltpu.HBM)
-            for array in (blocks.reshape(slots * bi * bj, bk), factor_b, factor_c)
+            for array in (coords.reshape(coords.shape[0]), blocks.reshape(slots * bi * bj, bk), factor_b, factor_c)
         ),
     )
 

time: 51.4 us -> 50.3 us (0.979)
  local copies, waits for them, and re-layouts: 2.66 us -> 2.01 us
    unnamed x5 -> x3, local copies, waits for them, and re-layouts: 2.66 us -> 2.01 us
where the time goes in v7:
time: 50.3 us; the launch traced here: 50.1 us
  Pallas kernels  47.5 us (94%)
  local copies, waits for them, and re-layouts  2.01 us (4%)
  between operations  0.64 us (1%)
    pallas_call x1, Pallas kernels, on_device(): pl.pallas_call(functools.partial(kernel, sizes), out_shape=shapes, in_spe...  47.5 us
    unnamed x3, local copies, waits for them, and re-layouts  2.01 us

profile of v7, /device:TPU:0, one launch (start us, length us, event | category | flops | bytes accessed | tf_op | source)
XLA Modules:
  0.0 50.1 jit_solution(17336285258456151299)
XLA Ops:
  0.6 47.5 %shard_map.67 = (f32[256,128]{1,0:T(8,128)S(1)}, f32[256,128]{1,0:T(8,128)S(1)}, f32[512,128]{1,0:T(8,128)S(1)}) custom-call(s32[3]{0:T(128)} %bitcast.3, bf16[4096,128]{1,0:T(8,128)(2,1)} %bitcast.2, f32[256,128]{1,0:T(8,128)} %factor_b_hbm.1, f32[512,128]{1,0:T(8,128)} %factor_c_hbm.1), custom_call_target="tpu_custom_call" | custom-call | tf_op jit(solution)/shard_map/pallas_call | solution.py:490
  48.1 0.7 %copy.10 = f32[256,128]{1,0:T(8,128)} copy(f32[256,128]{1,0:T(8,128)S(1)} %get-tuple-element.6) | data formatting | bytes 262144
  48.8 0.7 %copy.11 = f32[256,128]{1,0:T(8,128)} copy(f32[256,128]{1,0:T(8,128)S(1)} %get-tuple-element.7) | data formatting | bytes 262144
  49.4 0.7 %copy.12 = f32[512,128]{1,0:T(8,128)} copy(f32[512,128]{1,0:T(8,128)S(1)} %get-tuple-element.8) | data formatting | bytes 524288
